TPU v7x, 512 devices: a whole 4x4x16 slice. The times are simulated.
512 devices in a mesh: feature: 8 (over y_lo, x), latent: 64 (over z, y_hi, core).
Axes of the slice: x: 4, y: 4 (y_hi: 2, y_lo: 2; y = y_hi * 2 + y_lo), z: 16, core: 2. Of those that a mesh axis runs over, the one named last changes fastest.
Arguments:
- activations: bfloat16 [320, 2, 8192], P('latent', None, 'feature'), may hold values from -6 to 6
- targets: bfloat16 [320, 2, 8192], P('latent', None, 'feature'), may hold values from -6 to 6
- enc_weight: bfloat16 [2, 8192, 16384], P(None, 'feature', 'latent'), may hold values from -0.0625 to 0.0625
- enc_bias: float32 [2, 16384], P(None, 'latent'), may hold values from -5 to 5
- dec_weight: bfloat16 [3, 16384, 8192], P(None, 'latent', 'feature'), may hold values from -0.09375 to 0.09375
- top_blocks: int32 [320, 2, 16], replicated, may hold values from 0 to 127, as said below
- pair_mask: int32 [2, 2, 128], replicated, may hold values from 0 to 1, as said below
Outputs:
- recon: bfloat16 [320, 2, 8192], P('latent', None, 'feature')
- enc_grad: float32 [2, 8192, 16384], P(None, 'feature', 'latent')
Inputs may be any that keep to these rules, and one draw needn't show every extreme that they name: `top_blocks`: for each row and layer the 16 block numbers are distinct. pair_mask[s, t, b] is 1 where s equals t and 0 where s is after t.
All inputs are finite; a program needn't handle non-finite values.
Results may differ from a plain program's by a relative error of at most 0.0051.
Values may be sent and summed in bfloat16 or wider, within the bound.
A program may use at most 64 MiB of HBM per device.

v0:
```python
import math

import jax
import jax.numpy as jnp
from jax import lax
from jax.sharding import PartitionSpec as P

BLOCK = 128
ROWS = 320


def pair_index(source, later, layer_count):
    return source * layer_count - source * (source - 1) // 2 + later - source


def body(activations, targets, enc_weight, enc_bias, dec_weight, top_blocks, pair_mask):
    layer_count = enc_weight.shape[0]
    latent_share = enc_weight.shape[2]
    feature_share = dec_weight.shape[2]
    local_blocks = latent_share // BLOCK
    first_block = lax.axis_index("latent") * local_blocks
    block_ids = first_block + jnp.arange(local_blocks, dtype=jnp.int32)
    block_hits = jnp.any(top_blocks[..., None] == block_ids, axis=2)
    active = jnp.repeat(block_hits.astype(jnp.float32), BLOCK, axis=-1)
    mask_local = lax.dynamic_slice_in_dim(pair_mask, first_block, local_blocks, 2)
    pair_gate = jnp.repeat(mask_local.astype(jnp.float32), BLOCK, axis=-1)
    loss_scale = 1.0 / math.sqrt(ROWS)
    inputs_all = lax.all_gather(activations, "latent", axis=0, tiled=True)
    partial_pre = jnp.einsum(
        "rld,ldf->rlf", inputs_all, enc_weight, preferred_element_type=jnp.float32
    )
    preact = lax.psum(partial_pre, "feature") + enc_bias[None]
    latent_codes = (active * preact).astype(jnp.bfloat16)
    outputs = []
    for later in range(layer_count):
        summed = jnp.zeros((latent_codes.shape[0], feature_share), jnp.float32)
        for source in range(later + 1):
            gated = latent_codes[:, source] * pair_gate[source, later].astype(jnp.bfloat16)[None]
            summed = summed + jnp.dot(
                gated,
                dec_weight[pair_index(source, later, layer_count)],
                preferred_element_type=jnp.float32,
            )
        outputs.append(summed)
    decoded = lax.psum_scatter(jnp.stack(outputs, 1), "latent", scatter_dimension=0, tiled=True)
    recon_rows = decoded.astype(jnp.bfloat16)
    errors = (decoded - targets.astype(jnp.float32)).astype(jnp.bfloat16)
    err_piece = lax.all_gather(errors, "latent", axis=0, tiled=True)
    outputs = []
    for source in range(layer_count):
        summed = jnp.zeros((err_piece.shape[0], latent_share), jnp.float32)
        for later in range(source, layer_count):
            summed = summed + pair_gate[source, later][None] * jnp.einsum(
                "rd,fd->rf",
                err_piece[:, later],
                dec_weight[pair_index(source, later, layer_count)],
                preferred_element_type=jnp.float32,
            )
        outputs.append(summed)
    partial_grad = jnp.stack(outputs, 1)
    code_grad = lax.psum(partial_grad, "feature")
    pre_grad = (active * code_grad * loss_scale).astype(jnp.bfloat16)
    enc_grad = jnp.einsum("rld,rlf->ldf", inputs_all, pre_grad, preferred_element_type=jnp.float32)
    return (recon_rows, enc_grad)


def solution(mesh):
    in_specs = (
        P("latent", None, "feature"),
        P("latent", None, "feature"),
        P(None, "feature", "latent"),
        P(None, "latent"),
        P(None, "latent", "feature"),
        P(),
        P(),
    )
    out_specs = (P("latent", None, "feature"), P(None, "feature", "latent"))
    return jax.shard_map(body, mesh=mesh, in_specs=in_specs, out_specs=out_specs, check_vma=False)
```

profile of v0, /device:TPU:1, one launch (start us, length us, event | category | flops | bytes accessed | tf_op | source)
XLA Modules:
  0.0 1029.7 jit_solution(17412410955341866542)
XLA Ops:
  7.2 0.0 copy-start
  7.2 0.0 all-gather.3.cloned.1.call-start
  7.2 0.7 all-gather.3.cloned.1.call-update
  7.9 0.0 copy-start.3
  7.9 0.0 all-reduce.5.cloned.1.call-start
  8.0 150.0 %all-gather.3.cloned.1.call-done = bf16[320,2,1024]{2,1,0:T(2,128)(2,1)} async-done(((bf16[5,2,1024]{2,1,0:T(2,128)(2,1)}), bf16[320,2,1024]{2,1,0:T(2,128)(2,1)}) %all-gather.3.cloned.1.call-update) | async-done | bytes 1310736 | tf_op jit(solution)/shard_map/all_gather | solution.py:28
  158.0 0.0 copy-done
  158.0 2.7 convolution_bitcast_fusion.2
  160.7 0.0 all-reduce.5.cloned.1.call-update
  160.7 0.0 all-reduce.9.cloned.1.call-start
  160.8 0.0 copy-done.3
  160.8 0.1 compare_reduce_fusion
  160.9 0.0 copy-start.6
  160.9 0.0 copy-start.5
  160.9 0.2 copy.26
  161.1 0.8 broadcast_in_dim.4
  161.9 0.5 reshape.55
  162.4 0.0 copy-start.1
  162.5 0.0 copy-start.2
  162.5 0.1 dynamic-slice_convert_fusion.1
  162.6 0.1 broadcast_in_dim.5
  162.7 79.1 %all-reduce.5.cloned.1.call-done = f32[320,2,256]{2,0,1:T(8,128)} async-done(((f32[320,2,256]{2,0,1:T(8,128)}), f32[320,2,256]{2,0,1:T(8,128)}) %all-reduce.5.cloned.1.call-update) | async-done | bytes 655376 | tf_op jit(solution)/shard_map/psum | solution.py:32
  241.8 1.2 multiply_convert_fusion.1
  243.0 0.0 copy-done.2
  243.0 0.3 fusion.9
  243.4 0.0 copy-done.1
  243.4 0.3 convolution_bitcast_fusion.1
  243.7 0.3 fusion
  244.1 0.3 pad_maximum_fusion
  244.4 3.5 copy.28
  247.9 0.0 all-reduce.9.cloned.1.call-update
  248.0 0.0 all-gather.5.cloned.1.call-start
  248.0 1.3 dynamic-slice
  249.9 538.0 %all-reduce.9.cloned.1.call-done = f32[320,2,1024]{2,1,0:T(2,128)} async-done(((f32[320,2,1024]{2,1,0:T(2,128)}), f32[320,2,1024]{2,1,0:T(2,128)}) %all-reduce.9.cloned.1.call-update) | async-done | bytes 2621456
  787.9 1.4 subtract_convert_fusion
  789.4 0.0 all-gather.5.cloned.1.call-update
  789.4 0.0 all-reduce.7.cloned.1.call-start
  789.4 142.9 %all-gather.5.cloned.1.call-done = bf16[320,2,1024]{2,1,0:T(2,128)(2,1)} async-done(((bf16[5,2,1024]{2,1,0:T(2,128)(2,1)}), bf16[320,2,1024]{2,1,0:T(2,128)(2,1)}) %all-gather.5.cloned.1.call-update) | async-done | bytes 1310736 | tf_op jit(solution)/shard_map/all_gather | solution.py:48
  932.3 4.0 fusion.32
  936.3 0.4 fusion.1
  936.7 0.4 convolution_multiply_fusion.2
  937.1 0.4 fusion.3
  937.5 0.9 pad_maximum_fusion.1
  938.4 0.0 all-reduce.7.cloned.1.call-update
  938.4 1.4 dynamic-slice_convert_fusion
  939.8 79.0 %all-reduce.7.cloned.1.call-done = f32[320,2,256]{2,0,1:T(8,128)} async-done(((f32[320,2,256]{2,0,1:T(8,128)}), f32[320,2,256]{2,0,1:T(8,128)}) %all-reduce.7.cloned.1.call-update) | async-done | bytes 655376 | tf_op jit(solution)/shard_map/psum | solution.py:61
  1018.8 2.6 convolution_bitcast_fusion
  1021.4 1.8 copy.32
  (11 shorter events, 0.1 us)
Async XLA Ops:
  7.2 150.8 %copy-start = (bf16[2,1024,256]{2,1,0:T(8,128)(2,1)S(1)}, bf16[2,1024,256]{2,1,0:T(8,128)(2,1)}, u32[]{:S(2)}) copy-start(bf16[2,1024,256]{2,1,0:T(8,128)(2,1)} %param.9) | copy-start | bytes 3145732
  7.2 150.8 %all-gather.3.cloned.1.call-start = ((), (), s32[]{:S(2)}) async-start(), calls=%async_computation | async-start | bytes 1331200 | tf_op jit(solution)/shard_map/all_gather | solution.py:28
  7.9 152.8 %copy-start.3 = (s32[320,2,16]{0,2,1:T(8,128)S(1)}, s32[320,2,16]{0,2,1:T(8,128)}, u32[]{:S(2)}) copy-start(s32[320,2,16]{0,2,1:T(8,128)} %param.12) | copy-start | bytes 122884
  7.9 233.9 %all-reduce.5.cloned.1.call-start = ((), (), s32[]{:S(2)}) async-start(), calls=%async_computation.1 | async-start | bytes 1310720 | tf_op jit(solution)/shard_map/psum | solution.py:32
  160.7 627.2 %all-reduce.9.cloned.1.call-start = ((), (), s32[]{:S(2)}) async-start(), calls=%async_computation.4 | async-start | bytes 5242880
  160.9 1.6 copy-start.6
  160.9 80.9 %copy-start.5 = (f32[2,256]{1,0:T(2,128)S(1)}, f32[2,256]{1,0:T(2,128)}, u32[]{:S(2)}) copy-start(f32[2,256]{1,0:T(2,128)} %param.10) | copy-start | bytes 6148
  162.4 80.9 %copy-start.1 = (f32[320,2,256]{2,0,1:T(8,128)}, f32[320,2,256]{2,0,1:T(8,128)S(1)}, u32[]{:S(2)}) copy-start(f32[320,2,256]{2,0,1:T(8,128)S(1)} %reshape.55) | copy-start | bytes 1966084
  162.5 80.6 %copy-start.2 = (bf16[3,256,1024]{2,1,0:T(8,128)(2,1)S(1)}, bf16[3,256,1024]{2,1,0:T(8,128)(2,1)}, u32[]{:S(2)}) copy-start(bf16[3,256,1024]{2,1,0:T(8,128)(2,1)} %param.11) | copy-start | bytes 4718596
  247.9 540.0 %copy-start.4 = (bf16[5,2,1024]{2,1,0:T(2,128)(2,1)S(1)}, bf16[5,2,1024]{2,1,0:T(2,128)(2,1)}, u32[]{:S(2)}) copy-start(bf16[5,2,1024]{2,1,0:T(2,128)(2,1)} %param.8) | copy-start | bytes 61444
  248.0 684.3 %all-gather.5.cloned.1.call-start = ((), (), s32[]{:S(2)}) async-start(), calls=%async_computation.2 | async-start | bytes 1331200 | tf_op jit(solution)/shard_map/all_gather | solution.py:48
  789.4 229.4 %all-reduce.7.cloned.1.call-start = ((), (), s32[]{:S(2)}) async-start(), calls=%async_computation.3 | async-start | bytes 1310720 | tf_op jit(solution)/shard_map/psum | solution.py:61
Sparse Core Ops, SparseCore 0:
  11.2 146.7 all-gather.2
  161.5 80.2 all-reduce.4
  248.1 539.8 all-reduce.8
  792.1 140.1 all-gather.4
  938.5 80.2 all-reduce.6
where the time goes:
time: 1030 us
  waiting for transfers between devices  990 us (96%)
  between operations  14.6 us (1%)
  local copies, waits for them, and re-layouts  13.7 us (1%)
    unnamed x6, waiting for transfers between devices  539 us
    all_gather x1, waiting for transfers between devices, body(): inputs_all = lax.all_gather(activations, 'latent', axis=0, tiled=True)  150 us
    all_gather x1, waiting for transfers between devices, body(): err_piece = lax.all_gather(errors, 'latent', axis=0, tiled=True)  143 us
    psum x1, waiting for transfers between devices, body(): preact = lax.psum(partial_pre, 'feature') + enc_bias[None]  79.1 us
    psum x1, waiting for transfers between devices, body(): code_grad = lax.psum(partial_grad, 'feature')  79 us
  transfers between devices with their start and end apart: 5, of which 5 were waited for; matrix products, arithmetic and copies ran while one was open for 0% of the time, Pallas kernels for 0%

commit v1 on v0

v1 whole, which is shorter than its diff:
```python
import functools
import math

import jax
import jax.numpy as jnp
from jax import lax
from jax.experimental import pallas as pl
from jax.experimental.pallas import tpu as pltpu
from jax.sharding import PartitionSpec as P

BLOCK = 128
LANES = 128
F32 = jnp.float32
BF16 = jnp.bfloat16
MESH = pl.DeviceIdType.MESH


def kernel(
    nz, nf, scale,
    act, tgt, enc_hbm, bias, dec_hbm, mask, gate,
    recon, a_all, pre_grad,
    enc, dec, x1, x2, xf, err_all, pf, gf,
    s1, r1, codes, s2, r2,
    core_out, core_in, right_out, right_in, left_out, left_in, y_out, y_in,
    load_sem, ag_recv1, ag_recv2, ag_right, ag_left, ag_core, y_send, y_recv,
    f_send, f_recv, core_send, core_recv, rs_rs, rs_rr, rs_ls, rs_lr,
):
    feat = lax.axis_index("feature")
    lat = lax.axis_index("latent")
    core = lat % 2
    yh = (lat // 2) % 2
    z = lat // 4
    hr, hl = nz // 2, nz // 2 - 1
    rb = act.shape[0]
    rows = a_all.shape[1]
    depth = a_all.shape[2]
    chunks = depth // LANES
    stride = 2 * chunks
    latents = enc.shape[2]
    fb = 2 * rows // nf

    def block(zz, yy, cc):
        return (zz * 2 + yy) * 2 + cc

    def zmod(v):
        return (v + nz) % nz

    right = {"latent": block(zmod(z + 1), yh, core)}
    left = {"latent": block(zmod(z - 1), yh, core)}
    other_y = {"latent": block(z, 1 - yh, core)}
    other_core = {"latent": block(z, yh, 1 - core)}

    def peer(i):
        return (feat + i) % nf

    barrier = pltpu.get_barrier_semaphore()
    for device in (right, left, other_y, other_core):
        pl.semaphore_signal(barrier, inc=1, device_id=device, device_id_type=MESH)
    for i in range(1, nf):
        pl.semaphore_signal(barrier, inc=1, device_id={"feature": peer(i)}, device_id_type=MESH)

    load_enc = pltpu.make_async_copy(enc_hbm, enc, load_sem.at[0])
    load_dec = pltpu.make_async_copy(dec_hbm, dec, load_sem.at[1])
    load_enc.start()
    load_dec.start()
    x1[lat] = act[...]
    pl.semaphore_wait(barrier, 4 + nf - 1)

    def remote(src, dst, send, recv, device):
        return pltpu.make_async_remote_copy(
            src_ref=src, dst_ref=dst, send_sem=send, recv_sem=recv, device_id=device, device_id_type=MESH
        )

    def gather(x, recv):
        def copy(b, send, device):
            return remote(x.at[b], x.at[b], send.at[b // 4 * 2 + (b // 2) % 2], recv.at[b], device)

        def y_copy():
            return remote(x.at[lat], x.at[lat], y_send, recv.at[lat], other_y)

        def arrived(b):
            copy(b, ag_right, right).wait_recv()

        copy(lat, ag_right, right).start()
        copy(lat, ag_left, left).start()
        y_copy().start()
        copy(lat, ag_core, other_core).start()
        twin = block(z, 1 - yh, core)
        arrived(twin)
        copy(twin, ag_right, right).start()
        copy(twin, ag_left, left).start()
        copy(twin, ag_core, other_core).start()

        def step(s, carry):
            for yy in (yh, 1 - yh):
                from_left = block(zmod(z - s), yy, core)
                arrived(from_left)
                copy(from_left, ag_right, right).start()
                copy(from_left, ag_core, other_core).start()
                from_right = block(zmod(z + s), yy, core)
                arrived(from_right)

                @pl.when(s < hl)
                def _():
                    copy(from_right, ag_left, left).start()

                copy(from_right, ag_core, other_core).start()
            return carry

        lax.fori_loop(1, hl + 1, step, 0)
        for yy in (yh, 1 - yh):
            last = block(zmod(z - hr), yy, core)
            arrived(last)
            copy(last, ag_core, other_core).start()

        def finish(i, carry):
            arrived(i * 2 + 1 - core)
            copy(i * 2 + core, ag_core, other_core).wait_send()
            return carry

        lax.fori_loop(0, 2 * nz, finish, 0)

        def finish_sends(s, carry):
            for yy in (yh, 1 - yh):
                copy(block(zmod(z - s), yy, core), ag_right, right).wait_send()

                @pl.when(s < hl)
                def _():
                    copy(block(zmod(z + s), yy, core), ag_left, left).wait_send()
            return carry

        lax.fori_loop(0, hr, finish_sends, 0)
        y_copy().wait_send()

    def unpack(x, out):
        def widen(b, carry):
            xf[pl.ds(pl.multiple_of(b * rb, 8), rb), :] = x[b].astype(F32)
            return carry

        lax.fori_loop(0, 4 * nz, widen, 0)
        for layer in range(2):
            for k in range(chunks):
                out[layer, :, k * LANES:(k + 1) * LANES] = xf[
                    pl.ds(layer * chunks + k, rows, stride=stride), :
                ].astype(BF16)

    def exchange(src, dst, which, own_slot):
        def copy(j):
            return remote(
                src.at[feat if own_slot else j], dst.at[feat],
                f_send.at[which, j], f_recv.at[which, feat], {"feature": j},
            )

        for i in range(1, nf):
            copy(peer(i)).start()

        def wait_from(j):
            remote(src.at[j], dst.at[j], f_send.at[which, j], f_recv.at[which, j], {"feature": j}).wait_recv()

        def wait_sent():
            for i in range(1, nf):
                copy(peer(i)).wait_send()

        return wait_from, wait_sent

    def feature_sum(part, out, inbox, which):
        for j in range(nf):
            out[j] = part[j * fb:(j + 1) * fb, :].astype(BF16)
        wait_from, wait_sent = exchange(out, inbox, which, False)
        total = part[pl.ds(pl.multiple_of(feat * fb, 8), fb), :]
        for i in range(1, nf):
            wait_from(peer(i))
            total = total + inbox[peer(i)].astype(F32)
        wait_sent()
        return total

    def share(out, which):
        wait_from, wait_sent = exchange(out, out, which, True)
        for i in range(1, nf):
            wait_from(peer(i))
        wait_sent()

    gather(x1, ag_recv1)
    unpack(x1, a_all)
    load_enc.wait()
    for layer in range(2):
        pf[layer * rows:(layer + 1) * rows, :] = jnp.dot(a_all[layer], enc[layer], preferred_element_type=F32)
    total = feature_sum(pf, s1, r1, 0)
    codes[feat] = (mask[...] * (total + bias[...])).astype(BF16)
    share(codes, 1)

    half = nf // 2
    c0 = codes[0:half].reshape(rows, latents)
    c1 = codes[half:nf].reshape(rows, latents)
    c01 = (c0.astype(F32) * gate[...]).astype(BF16)
    load_dec.wait()
    wide = 2 * LANES
    for n in range(depth // wide):
        cols = slice(n * wide, (n + 1) * wide)
        d0 = jnp.dot(c0, dec[0, :, cols], preferred_element_type=F32)
        d1 = jnp.dot(c01, dec[1, :, cols], preferred_element_type=F32)
        d1 = d1 + jnp.dot(c1, dec[2, :, cols], preferred_element_type=F32)
        for k in range(2):
            lanes = slice(k * LANES, (k + 1) * LANES)
            xf[pl.ds(2 * n + k, rows, stride=stride), :] = d0[:, lanes]
            xf[pl.ds(chunks + 2 * n + k, rows, stride=stride), :] = d1[:, lanes]

    def local(b):
        return xf[pl.ds(pl.multiple_of(b * rb, 8), rb), :]

    def core_copy(d):
        return remote(core_out.at[d], core_in.at[d], core_send.at[d], core_recv.at[d], other_core)

    def send_core(d):
        for yy in range(2):
            core_out[d, yy] = local(block(d, yy, 1 - core)).astype(BF16)
        core_copy(d).start()

    def send_cores(s, carry):
        send_core(zmod(z + hr + 1 - s))

        @pl.when(s <= hl)
        def _():
            send_core(zmod(z - hl - 1 + s))
        return carry

    lax.fori_loop(1, hr + 1, send_cores, 0)
    send_core(z)

    def right_copy(s, yy):
        return remote(right_out.at[s, yy], right_in.at[s, yy], rs_rs.at[s, yy], rs_rr.at[s, yy], right)

    def left_copy(s, yy):
        return remote(left_out.at[s, yy], left_in.at[s, yy], rs_ls.at[s, yy], rs_lr.at[s, yy], left)

    def ring(s, d, copy, out, into):
        core_copy(d).wait_recv()
        for yy in range(2):
            value = local(block(d, yy, core)) + core_in[d, yy].astype(F32)

            @pl.when(s == 0)
            def _():
                out[s, yy] = value.astype(BF16)

            @pl.when(s > 0)
            def _():
                copy(s - 1, yy).wait_recv()
                out[s, yy] = (value + into[s - 1, yy].astype(F32)).astype(BF16)

            copy(s, yy).start()

    def ring_step(s, carry):
        ring(s, zmod(z + hr - s), right_copy, right_out, right_in)

        @pl.when(s < hl)
        def _():
            ring(s, zmod(z - hl + s), left_copy, left_out, left_in)
        return carry

    lax.fori_loop(0, hr, ring_step, 0)
    core_copy(z).wait_recv()
    for yy in range(2):
        right_copy(hr - 1, yy).wait_recv()
        left_copy(hl - 1, yy).wait_recv()

    def final(yy):
        value = local(block(z, yy, core)) + core_in[z, yy].astype(F32)
        return value + right_in[hr - 1, yy].astype(F32) + left_in[hl - 1, yy].astype(F32)

    y_out[...] = final(1 - yh)
    y_copy = remote(y_out, y_in, y_send, y_recv, other_y)
    y_copy.start()
    mine = final(yh)
    y_copy.wait_recv()
    decoded = mine + y_in[...]
    recon[...] = decoded.astype(BF16)
    x2[lat] = (decoded - tgt[...].astype(F32)).astype(BF16)
    y_copy.wait_send()

    def finish_cores(d, carry):
        core_copy(d).wait_send()
        return carry

    lax.fori_loop(0, nz, finish_cores, 0)

    def finish_ring(s, carry):
        for yy in range(2):
            right_copy(s, yy).wait_send()

            @pl.when(s < hl)
            def _():
                left_copy(s, yy).wait_send()
        return carry

    lax.fori_loop(0, hr, finish_ring, 0)

    gather(x2, ag_recv2)
    unpack(x2, err_all)
    across = (((1,), (1,)), ((), ()))
    g0 = lax.dot_general(err_all[0], dec[0], across, preferred_element_type=F32)
    g01 = lax.dot_general(err_all[1], dec[1], across, preferred_element_type=F32)
    gf[0:rows, :] = g0 + gate[...] * g01
    gf[rows:2 * rows, :] = lax.dot_general(err_all[1], dec[2], across, preferred_element_type=F32)
    total = feature_sum(gf, s2, r2, 2)
    pre_grad[feat] = (mask[...] * total * scale).astype(BF16)
    share(pre_grad, 3)


def body(nz, nf, activations, targets, enc_weight, enc_bias, dec_weight, top_blocks, pair_mask):
    own_rows, layers, depth = activations.shape
    rows = top_blocks.shape[0]
    latents = enc_weight.shape[2]
    local_blocks = latents // BLOCK
    chunks = depth // LANES
    rb = own_rows * layers * chunks
    fb = layers * rows // nf
    first_block = lax.axis_index("latent") * local_blocks
    feat = lax.axis_index("feature")
    block_ids = first_block + jnp.arange(local_blocks, dtype=jnp.int32)
    top = lax.dynamic_slice_in_dim(top_blocks.transpose(1, 0, 2).reshape(layers * rows, -1), feat * fb, fb, 0)
    hits = jnp.any(top[..., None] == block_ids, axis=1)
    mask = jnp.repeat(hits.astype(F32), BLOCK, axis=-1)
    gate = lax.dynamic_slice_in_dim(pair_mask[0, 1], first_block, local_blocks, 0)
    gate = jnp.repeat(gate.astype(F32), BLOCK)[None]
    bias = lax.dynamic_slice_in_dim(enc_bias, feat * layers // nf, 1, 0)
    hr, hl = nz // 2, nz // 2 - 1
    blocks = 4 * nz
    vmem = pl.BlockSpec(memory_space=pltpu.VMEM)
    hbm = pl.BlockSpec(memory_space=pl.ANY)
    dma = pltpu.SemaphoreType.DMA
    recon, a_all, pre_grad = pl.pallas_call(
        functools.partial(kernel, nz, nf, 1.0 / math.sqrt(rows)),
        out_shape=(
            jax.ShapeDtypeStruct((rb, LANES), BF16),
            jax.ShapeDtypeStruct((layers, rows, depth), BF16),
            jax.ShapeDtypeStruct((nf, fb, latents), BF16),
        ),
        in_specs=[vmem, vmem, hbm, vmem, hbm, vmem, vmem],
        out_specs=(vmem, vmem, vmem),
        scratch_shapes=[
            pltpu.VMEM(enc_weight.shape, BF16),
            pltpu.VMEM(dec_weight.shape, BF16),
            pltpu.VMEM((blocks, rb, LANES), BF16),
            pltpu.VMEM((blocks, rb, LANES), BF16),
            pltpu.VMEM((blocks * rb, LANES), F32),
            pltpu.VMEM((layers, rows, depth), BF16),
            pltpu.VMEM((layers * rows, latents), F32),
            pltpu.VMEM((layers * rows, latents), F32),
            pltpu.VMEM((nf, fb, latents), BF16),
            pltpu.VMEM((nf, fb, latents), BF16),
            pltpu.VMEM((nf, fb, latents), BF16),
            pltpu.VMEM((nf, fb, latents), BF16),
            pltpu.VMEM((nf, fb, latents), BF16),
            pltpu.VMEM((nz, 2, rb, LANES), BF16),
            pltpu.VMEM((nz, 2, rb, LANES), BF16),
            pltpu.VMEM((hr, 2, rb, LANES), BF16),
            pltpu.VMEM((hr, 2, rb, LANES), BF16),
            pltpu.VMEM((hl, 2, rb, LANES), BF16),
            pltpu.VMEM((hl, 2, rb, LANES), BF16),
            pltpu.VMEM((rb, LANES), F32),
            pltpu.VMEM((rb, LANES), F32),
            dma((2,)),
            dma((blocks,)),
            dma((blocks,)),
            dma((2 * nz,)),
            dma((2 * nz,)),
            dma((2 * nz,)),
            dma,
            dma,
            dma((4, nf)),
            dma((4, nf)),
            dma((nz,)),
            dma((nz,)),
            dma((hr, 2)),
            dma((hr, 2)),
            dma((hl, 2)),
            dma((hl, 2)),
        ],
        compiler_params=pltpu.CompilerParams(
            collective_id=0, has_side_effects=True, vmem_limit_bytes=48 * 2**20
        ),
    )(
        activations.reshape(rb, LANES), targets.reshape(rb, LANES), enc_weight, bias, dec_weight, mask, gate
    )
    enc_grad = jnp.einsum(
        "lrd,lrf->ldf", a_all, pre_grad.reshape(layers, rows, latents), preferred_element_type=F32
    )
    return recon.reshape(own_rows, layers, depth), enc_grad


def solution(mesh):
    in_specs = (
        P("latent", None, "feature"),
        P("latent", None, "feature"),
        P(None, "feature", "latent"),
        P(None, "latent"),
        P(None, "latent", "feature"),
        P(),
        P(),
    )
    out_specs = (P("latent", None, "feature"), P(None, "feature", "latent"))
    step = functools.partial(body, mesh.shape["latent"] // 4, mesh.shape["feature"])
    return jax.shard_map(step, mesh=mesh, in_specs=in_specs, out_specs=out_specs, check_vma=False)
```

time: 1030 us -> 147 us (0.14)
  waiting for transfers between devices: 990 us -> 0 us
  Pallas kernels: 0 us -> 136 us
  between operations: 14.6 us -> 0.71 us
    unnamed x6 -> x0, waiting for transfers between devices: 539 us -> none
    all_gather x2 -> x0, waiting for transfers between devices: 293 us -> none  [the longest x1 150 us: body(): inputs_all = lax.all_gather(activations, 'latent', axis=0, tiled=True)]
    psum x2 -> x0, waiting for transfers between devices: 158 us -> none  [the longest x1 79.1 us: body(): preact = lax.psum(partial_pre, 'feature') + enc_bias[None]]
    pallas_call x0 -> x1, Pallas kernels: none -> 136 us  [body(): pl.pallas_call(functools.partial(kernel, nz, nf, 1.0 / math.sqrt(rows)),...]
  transfers between devices with their start and end apart: 5 -> 0, of which waited for: 5 -> 0; matrix products, arithmetic and copies ran while one was open for 0% -> 0% of each run, Pallas kernels for 0% -> 0%
where the time goes in v1:
time: 147 us; the launch traced here: 146 us
  Pallas kernels  136 us (93%)
  local copies, waits for them, and re-layouts  7.39 us (5%)
  matrix products  2.15 us (1%)
    pallas_call x1, Pallas kernels, body(): pl.pallas_call(functools.partial(kernel, nz, nf, 1.0 / math.sqrt(rows)),...  136 us
    unnamed x7, local copies, waits for them, and re-layouts  3.28 us

profile of v1, /device:TPU:1, one launch (start us, length us, event | category | flops | bytes accessed | tf_op | source)
XLA Modules:
  0.0 146.4 jit_solution(15204722992319165859)
XLA Ops:
  0.6 0.0 copy-start
  0.7 0.6 copy-done
  1.3 0.7 slice.3
  2.0 0.1 fusion.1
  2.1 0.1 broadcast_in_dim.9
  2.2 0.7 reshape.29.act
  2.9 0.7 reshape.30.tgt
  3.7 0.8 copy.11
  4.5 0.1 reshape.31
  4.6 0.1 constant_dynamic-slice_fusion.1
  4.7 0.1 compare_reduce_fusion
  4.8 0.1 copy.12
  4.9 0.1 broadcast_in_dim.8
  5.0 0.0 copy-start.1
  5.0 1.4 copy-done.1
  6.4 0.0 copy-start.2
  6.4 1.2 copy-done.2
  7.7 136.0 %shard_map.86 = (bf16[80,128]{1,0:T(8,128)(2,1)S(1)}, bf16[2,320,1024]{2,1,0:T(8,128)(2,1)S(1)}, bf16[8,80,256]{2,1,0:T(8,128)(2,1)S(1)}) custom-call(bf16[80,128]{1,0:T(8,128)(2,1)S(1)} %reshape.29.act, bf16[80,128]{1,0:T(8,128)(2,1)S(1)} %reshape.30.tgt, bf16[2,1024,256]{2,1,0:T(8,128)(2,1)S(1)} %copy-done.2, ...), custom_call_target="tpu_custom_call" | custom-call | tf_op jit(solution)/shard_map/pallas_call | solution.py:331
  143.7 0.6 reshape.33
  144.3 2.1 %fusion.2 = f32[2,1024,256]{2,1,0:T(8,128)} fusion(bf16[2,320,1024]{2,1,0:T(8,128)(2,1)S(1)} %get-tuple-element.6, bf16[2,320,256]{2,1,0:T(8,128)(2,1)S(1)} %bitcast.13), kind=kOutput, calls=%fused_computation.8 | convolution fusion | flops 335544320 | bytes 3735552 | tf_op jit(solution)/shard_map/lrd,lrf->ldf/dot_general | solution.py:385
  (4 shorter events, 0.0 us)
Async XLA Ops:
  0.6 0.7 copy-start
  5.0 1.4 copy-start.1
  6.4 1.2 copy-start.2

commit v2 on v0

v2 whole, which is shorter than its diff:
```python
import functools
import math

import jax
import jax.numpy as jnp
from jax import lax
from jax.experimental import pallas as pl
from jax.experimental.pallas import tpu as pltpu
from jax.sharding import PartitionSpec as P

BLOCK = 128
LANES = 128
F32 = jnp.float32
BF16 = jnp.bfloat16
MESH = pl.DeviceIdType.MESH
NEAR = 4
MESSAGES = (
    (1, 0, "all", 0), (1, 1, "all", 1), (-1, 0, "all", 2), (-1, 1, "all", 3),
    (2, 0, "low", 4), (2, 1, "low", 5), (-2, 0, "high", 4), (-2, 1, "high", 5),
    (0, 1, "all", 6),
)
SLOTS = 7


def kernel(
    nz, nf, scale,
    act, tgt, enc_hbm, bias, dec_hbm, mask, gate,
    recon, a_all, pre_out,
    enc, dec, x, xf, err_all, part, grad,
    f_out, f_in, codes, pre_grad,
    core_out, core_in, near_out, near_in, total, far_out, far_in,
    load_sem, far_s, far_r, near_s, near_r, core_s, core_r,
    f_send, f_recv, rc_s, rc_r, rn_s, rn_r, rf_s, rf_r,
):
    feat = lax.axis_index("feature")
    lat = lax.axis_index("latent")
    c = lat % 2
    y = (lat // 2) % 2
    z = lat // 4
    nq = nz // NEAR
    q, m = z // NEAR, z % NEAR
    rb = act.shape[1]
    rows, depth = a_all.shape[1:]
    chunks = depth // LANES
    latents = enc.shape[2]
    fb = rows // nf
    group = nq * rb

    def at(zz, yy, cc):
        return {"latent": (((zz + nz) % nz) * 2 + yy) * 2 + cc}

    other_core = at(z, y, 1 - c)
    near_devices = [at(z + dz, 1 - y if dy else y, c) for dz, dy, _, _ in MESSAGES]
    far_devices = [at(z + NEAR * j, y, c) for j in range(1, nq)]
    parts = {"all": slice(0, nq), "low": slice(0, nq // 2), "high": slice(nq // 2, nq)}

    def span(which):
        s = parts[which]
        return pl.ds(s.start, s.stop - s.start)

    def peer(i):
        return (feat + i) % nf

    feature_devices = [{"feature": peer(i)} for i in range(1, nf)]
    everyone = [other_core] + near_devices + far_devices + feature_devices
    barrier = pltpu.get_barrier_semaphore()
    for device in everyone:
        pl.semaphore_signal(barrier, inc=1, device_id=device, device_id_type=MESH)
    load_enc = pltpu.make_async_copy(enc_hbm, enc, load_sem.at[0])
    load_dec = pltpu.make_async_copy(dec_hbm, dec, load_sem.at[1])
    load_enc.start()
    load_dec.start()
    for t in range(2):
        x[0, t, m, y, c, q] = act[t]
    pl.semaphore_wait(barrier, len(everyone))

    def remote(src, dst, send, recv, device):
        return pltpu.make_async_remote_copy(
            src_ref=src, dst_ref=dst, send_sem=send, recv_sem=recv, device_id=device, device_id_type=MESH
        )

    def far_copy(g, t, j):
        ref = x.at[g, t, m, y, c, q]
        return remote(ref, ref, far_s.at[g, t, j], far_r.at[g, t, j], far_devices[j - 1])

    def far_arrival(g, t, j):
        ref = x.at[g, t, m, y, c, (q - j + nq) % nq]
        return remote(ref, ref, far_s.at[g, t, j], far_r.at[g, t, j], far_devices[j - 1])

    def near_copy(g, t, n):
        ref = x.at[g, t, m, y, c, span(MESSAGES[n][2])]
        return remote(ref, ref, near_s.at[g, t, n], near_r.at[g, t, n], near_devices[n])

    def arrival_ref(g, t, n, cc):
        if n == len(MESSAGES):
            return x.at[g, t, m, y, cc]
        dz, dy, which, _ = MESSAGES[n]
        return x.at[g, t, (m - dz + NEAR) % NEAR, 1 - y if dy else y, cc, span(which)]

    def near_arrival(g, t, n):
        ref = arrival_ref(g, t, n, c)
        return remote(ref, ref, near_s.at[g, t, n], near_r.at[g, t, n], near_devices[n])

    def core_copy(g, t, n, cc):
        ref = arrival_ref(g, t, n, cc)
        return remote(ref, ref, core_s.at[g, t, n], core_r.at[g, t, n], other_core)

    def gather_far(g, t):
        for j in range(1, nq):
            far_copy(g, t, j).start()

    def gather_near(g, t):
        for j in range(1, nq):
            far_arrival(g, t, j).wait_recv()
        for n in range(len(MESSAGES)):
            near_copy(g, t, n).start()
        core_copy(g, t, len(MESSAGES), c).start()

    def gather_core(g, t):
        for n in range(len(MESSAGES)):
            near_arrival(g, t, n).wait_recv()
            core_copy(g, t, n, c).start()

    def gather_end(g, t, out):
        for n in range(len(MESSAGES) + 1):
            core_copy(g, t, n, 1 - c).wait_recv()

        def widen(i, carry):
            blocks = x[g, t, i // 4, (i // 2) % 2, i % 2].astype(F32)
            xf[t, pl.ds(pl.multiple_of(i * group, 8), group), :] = blocks.reshape(group, LANES)
            return carry

        lax.fori_loop(0, 4 * NEAR, widen, 0)
        for k in range(chunks):
            out[t, :, k * LANES:(k + 1) * LANES] = xf[t, pl.ds(k, rows, stride=chunks), :].astype(BF16)

    def gather_sent(g, t):
        for j in range(1, nq):
            far_copy(g, t, j).wait_send()
        for n in range(len(MESSAGES)):
            near_copy(g, t, n).wait_send()
        for n in range(len(MESSAGES) + 1):
            core_copy(g, t, n, c).wait_send()

    def sum_copy(g, t, i):
        j = peer(i)
        return remote(
            f_out.at[g, t, j], f_in.at[g, t, i], f_send.at[0, g, t, i], f_recv.at[0, g, t, i], feature_devices[i - 1]
        )

    def sum_start(g, t, values):
        for j in range(nf):
            f_out[g, t, j] = values[t, j * fb:(j + 1) * fb, :].astype(BF16)
        for i in range(1, nf):
            sum_copy(g, t, i).start()

    def sum_end(g, t, values):
        acc = values[t, pl.ds(pl.multiple_of(feat * fb, 8), fb), :]
        for i in range(1, nf):
            sum_copy(g, t, i).wait_recv()
            acc = acc + f_in[g, t, i].astype(F32)
        return acc

    def share_copy(g, t, ref, i, mine):
        slot = ref.at[t, feat if mine else (feat - i + nf) % nf]
        return remote(slot, slot, f_send.at[1, g, t, i], f_recv.at[1, g, t, i], feature_devices[i - 1])

    def share_start(g, t, ref):
        for i in range(1, nf):
            share_copy(g, t, ref, i, True).start()

    def share_end(g, t, ref):
        for i in range(1, nf):
            share_copy(g, t, ref, i, False).wait_recv()

    def feature_sent(g, t, ref):
        for i in range(1, nf):
            sum_copy(g, t, i).wait_send()
            share_copy(g, t, ref, i, True).wait_send()

    def local(t, mm, yy, cc):
        start = ((mm * 2 + yy) * 2 + cc) * group
        return xf[t, pl.ds(pl.multiple_of(start, 8), group), :]

    def blocks(value):
        return value.reshape(nq, rb, LANES)

    steps = (1, -1, 2, 0)

    def rc_copy(t, s):
        mm = (m + steps[s] + NEAR) % NEAR
        return remote(core_out.at[t, mm], core_in.at[t, mm], rc_s.at[t, s], rc_r.at[t, s], other_core)

    def reduce_core(t):
        for s in range(NEAR):
            mm = (m + steps[s] + NEAR) % NEAR
            for yy in range(2):
                core_out[t, mm, yy] = blocks(local(t, mm, yy, 1 - c)).astype(BF16)
            rc_copy(t, s).start()

    def with_core(t, mm, yy):
        return blocks(local(t, mm, yy, c)) + core_in[t, mm, yy].astype(F32)

    def rn_copy(t, n):
        dz, dy, which, slot = MESSAGES[n]
        mm = (m + dz + NEAR) % NEAR
        yy = 1 - y if dy else y
        return remote(
            near_out.at[t, mm, yy, span(which)], near_in.at[t, slot, span(which)],
            rn_s.at[t, n], rn_r.at[t, n], near_devices[n],
        )

    def reduce_near(t):
        for s, messages in enumerate(((0, 1), (2, 3), (4, 5, 6, 7), (8,))):
            mm = (m + steps[s] + NEAR) % NEAR
            rc_copy(t, s).wait_recv()
            for yy in ((y, 1 - y) if s < 3 else (1 - y,)):
                near_out[t, mm, yy] = with_core(t, mm, yy).astype(BF16)
            for n in messages:
                rn_copy(t, n).start()

    def rf_copy(t, j):
        return remote(far_out.at[t, j], far_in.at[t, j], rf_s.at[t, j], rf_r.at[t, j], far_devices[j - 1])

    def reduce_far(t):
        for n in range(len(MESSAGES)):
            rn_copy(t, n).wait_recv()
        acc = with_core(t, m, y)
        for slot in range(SLOTS):
            acc = acc + near_in[t, slot].astype(F32)
        total[t] = acc
        for j in range(1, nq):
            far_out[t, j] = total[t, (q + j) % nq].astype(BF16)
            rf_copy(t, j).start()

    def reduce_end(t):
        acc = total[t, q]
        for j in range(1, nq):
            rf_copy(t, j).wait_recv()
            acc = acc + far_in[t, j].astype(F32)
        recon[t] = acc.astype(BF16)
        x[1, t, m, y, c, q] = (acc - tgt[t].astype(F32)).astype(BF16)

    def reduce_sent(t):
        for s in range(NEAR):
            rc_copy(t, s).wait_send()
        for n in range(len(MESSAGES)):
            rn_copy(t, n).wait_send()
        for j in range(1, nq):
            rf_copy(t, j).wait_send()

    both = (0, 1)
    for t in both:
        gather_far(0, t)
    for t in both:
        gather_near(0, t)
    load_enc.wait()
    for t in both:
        gather_core(0, t)
    for t in both:
        gather_end(0, t, a_all)
        part[t] = jnp.dot(a_all[t], enc[t], preferred_element_type=F32)
        sum_start(0, t, part)
    for t in both:
        codes[t, feat] = (mask[t] * (sum_end(0, t, part) + bias[t:t + 1, :])).astype(BF16)
        share_start(0, t, codes)
    load_dec.wait()

    def whole(t):
        return codes[t].astype(F32).reshape(rows, latents)

    wide = 2 * LANES
    for t in both:
        share_end(0, t, codes)
        if t == 0:
            terms = ((whole(0).astype(BF16), 0),)
        else:
            terms = (((whole(0) * gate[...]).astype(BF16), 1), (whole(1).astype(BF16), 2))
        for n in range(depth // wide):
            cols = slice(n * wide, (n + 1) * wide)
            value = sum(jnp.dot(code, dec[p, :, cols], preferred_element_type=F32) for code, p in terms)
            for k in range(2):
                xf[t, pl.ds(2 * n + k, rows, stride=chunks), :] = value[:, k * LANES:(k + 1) * LANES]
        reduce_core(t)
    for t in both:
        reduce_near(t)
    for t in both:
        gather_sent(0, t)
        feature_sent(0, t, codes)
    for t in both:
        reduce_far(t)
    for t in both:
        reduce_end(t)
        gather_far(1, t)
    for t in both:
        gather_near(1, t)
    for t in both:
        reduce_sent(t)
    for t in both:
        gather_core(1, t)
    across = (((1,), (1,)), ((), ()))
    gather_end(1, 0, err_all)
    grad[0] = lax.dot_general(err_all[0], dec[0], across, preferred_element_type=F32)
    gather_end(1, 1, err_all)
    grad[1] = lax.dot_general(err_all[1], dec[2], across, preferred_element_type=F32)
    sum_start(1, 1, grad)
    grad[0] = grad[0] + gate[...] * lax.dot_general(err_all[1], dec[1], across, preferred_element_type=F32)
    sum_start(1, 0, grad)
    for t in (1, 0):
        pre_grad[t, feat] = (mask[t] * sum_end(1, t, grad) * scale).astype(BF16)
        share_start(1, t, pre_grad)
    for t in both:
        gather_sent(1, t)
    for t in (1, 0):
        share_end(1, t, pre_grad)
        pre_out[t] = pre_grad[t].astype(F32).reshape(rows, latents).astype(BF16)
    for t in both:
        feature_sent(1, t, pre_grad)


def body(nz, nf, activations, targets, enc_weight, enc_bias, dec_weight, top_blocks, pair_mask):
    own_rows, layers, depth = activations.shape
    rows = top_blocks.shape[0]
    latents = enc_weight.shape[2]
    local_blocks = latents // BLOCK
    chunks = depth // LANES
    rb = own_rows * chunks
    fb = rows // nf
    nq = nz // NEAR
    first_block = lax.axis_index("latent") * local_blocks
    feat = lax.axis_index("feature")
    block_ids = first_block + jnp.arange(local_blocks, dtype=jnp.int32)
    top = top_blocks.reshape(nq, NEAR, 2, 2, own_rows, layers, -1).transpose(5, 1, 2, 3, 0, 4, 6)
    top = lax.dynamic_slice_in_dim(top.reshape(layers, rows, -1), feat * fb, fb, 1)
    hits = jnp.any(top[..., None] == block_ids, axis=2)
    mask = jnp.repeat(hits.astype(F32), BLOCK, axis=-1)
    gate = lax.dynamic_slice_in_dim(pair_mask[0, 1], first_block, local_blocks, 0)
    gate = jnp.repeat(gate.astype(F32), BLOCK)[None]
    vmem = pl.BlockSpec(memory_space=pltpu.VMEM)
    hbm = pl.BlockSpec(memory_space=pl.ANY)
    dma = pltpu.SemaphoreType.DMA
    bf, f32 = (lambda *s: pltpu.VMEM(s, BF16)), (lambda *s: pltpu.VMEM(s, F32))
    count = len(MESSAGES)
    recon, a_all, pre_grad = pl.pallas_call(
        functools.partial(kernel, nz, nf, 1.0 / math.sqrt(rows)),
        out_shape=(
            jax.ShapeDtypeStruct((layers, rb, LANES), BF16),
            jax.ShapeDtypeStruct((layers, rows, depth), BF16),
            jax.ShapeDtypeStruct((layers, rows, latents), BF16),
        ),
        in_specs=[vmem, vmem, hbm, vmem, hbm, vmem, vmem],
        out_specs=(vmem, vmem, vmem),
        scratch_shapes=[
            bf(*enc_weight.shape),
            bf(*dec_weight.shape),
            bf(2, layers, NEAR, 2, 2, nq, rb, LANES),
            f32(layers, rows * chunks, LANES),
            bf(layers, rows, depth),
            f32(layers, rows, latents),
            f32(layers, rows, latents),
            bf(2, layers, nf, fb, latents),
            bf(2, layers, nf, fb, latents),
            bf(layers, nf, fb, latents),
            bf(layers, nf, fb, latents),
            bf(layers, NEAR, 2, nq, rb, LANES),
            bf(layers, NEAR, 2, nq, rb, LANES),
            bf(layers, NEAR, 2, nq, rb, LANES),
            bf(layers, SLOTS, nq, rb, LANES),
            f32(layers, nq, rb, LANES),
            bf(layers, nq, rb, LANES),
            bf(layers, nq, rb, LANES),
            dma((2,)),
            dma((2, layers, nq)),
            dma((2, layers, nq)),
            dma((2, layers, count)),
            dma((2, layers, count)),
            dma((2, layers, count + 1)),
            dma((2, layers, count + 1)),
            dma((2, 2, layers, nf)),
            dma((2, 2, layers, nf)),
            dma((layers, NEAR)),
            dma((layers, NEAR)),
            dma((layers, count)),
            dma((layers, count)),
            dma((layers, nq)),
            dma((layers, nq)),
        ],
        compiler_params=pltpu.CompilerParams(
            collective_id=0, has_side_effects=True, vmem_limit_bytes=48 * 2**20
        ),
    )(
        activations.transpose(1, 0, 2).reshape(layers, rb, LANES),
        targets.transpose(1, 0, 2).reshape(layers, rb, LANES),
        enc_weight, enc_bias, dec_weight, mask, gate,
    )
    enc_grad = jnp.einsum("lrd,lrf->ldf", a_all, pre_grad, preferred_element_type=F32)
    return recon.reshape(layers, own_rows, depth).transpose(1, 0, 2), enc_grad


def solution(mesh):
    in_specs = (
        P("latent", None, "feature"),
        P("latent", None, "feature"),
        P(None, "feature", "latent"),
        P(None, "latent"),
        P(None, "latent", "feature"),
        P(),
        P(),
    )
    out_specs = (P("latent", None, "feature"), P(None, "feature", "latent"))
    step = functools.partial(body, mesh.shape["latent"] // 4, mesh.shape["feature"])
    return jax.shard_map(step, mesh=mesh, in_specs=in_specs, out_specs=out_specs, check_vma=False)
```

time: 1030 us -> 106 us (0.10)
  waiting for transfers between devices: 990 us -> 0 us
  Pallas kernels: 0 us -> 96.4 us
  between operations: 14.6 us -> 0.75 us
    unnamed x6 -> x0, waiting for transfers between devices: 539 us -> none
    all_gather x2 -> x0, waiting for transfers between devices: 293 us -> none  [the longest x1 150 us: body(): inputs_all = lax.all_gather(activations, 'latent', axis=0, tiled=True)]
    psum x2 -> x0, waiting for transfers between devices: 158 us -> none  [the longest x1 79.1 us: body(): preact = lax.psum(partial_pre, 'feature') + enc_bias[None]]
    pallas_call x0 -> x1, Pallas kernels: none -> 96.4 us  [body(): pl.pallas_call(functools.partial(kernel, nz, nf, 1.0 / math.sqrt(rows)),...]
  transfers between devices with their start and end apart: 5 -> 0, of which waited for: 5 -> 0; matrix products, arithmetic and copies ran while one was open for 0% -> 0% of each run, Pallas kernels for 0% -> 0%
where the time goes in v2:
time: 106 us; the launch traced here: 105 us
  Pallas kernels  96.4 us (91%)
  local copies, waits for them, and re-layouts  5.75 us (5%)
  matrix products  2.14 us (2%)
    pallas_call x1, Pallas kernels, body(): pl.pallas_call(functools.partial(kernel, nz, nf, 1.0 / math.sqrt(rows)),...  96.4 us
    unnamed x8, local copies, waits for them, and re-layouts  2.83 us
    dot_general x1, matrix products, body(): jnp.einsum('lrd,lrf->ldf', a_all, pre_grad, preferred_element_type=F32)  2.14 us

profile of v2, /device:TPU:1, one launch (start us, length us, event | category | flops | bytes accessed | tf_op | source)
XLA Modules:
  0.0 105.2 jit_solution(11135013296187765232)
XLA Ops:
  0.6 0.0 copy-start
  0.6 0.0 copy-start.2
  0.7 0.8 slice.3
  1.5 0.1 convert_bitcast_fusion
  1.5 0.1 broadcast_in_dim.9
  1.6 0.7 copy.18
  2.4 0.7 copy.19
  3.2 1.0 copy.20
  4.2 0.1 copy.22
  4.3 0.1 compare_reduce_fusion
  4.4 0.1 copy.23
  4.5 0.1 broadcast_in_dim.8
  4.7 0.1 reshape.33.mask
  4.7 0.0 copy-done
  4.8 0.0 copy-done.2
  4.8 0.0 copy-start.1
  4.8 1.2 %copy-done.1 = bf16[2,1024,256]{2,1,0:T(8,128)(2,1)S(1)} copy-done((bf16[2,1024,256]{2,1,0:T(8,128)(2,1)S(1)}, bf16[2,1024,256]{2,1,0:T(8,128)(2,1)}, u32[]{:S(2)}) %copy-start.1) | copy-done | bytes 1048600
  6.0 96.4 %shard_map.86 = (bf16[2,40,128]{2,1,0:T(8,128)(2,1)S(1)}, bf16[2,320,1024]{2,1,0:T(8,128)(2,1)S(1)}, bf16[2,320,256]{2,1,0:T(8,128)(2,1)S(1)}) custom-call(bf16[2,40,128]{2,1,0:T(8,128)(2,1)S(1)} %reshape.29.act, bf16[2,40,128]{2,1,0:T(8,128)(2,1)S(1)} %reshape.30.tgt, bf16[2,1024,256]{2,1,0:T(8,128)(2,1)S(1)} %copy-done.1, f32[2,256]{1,0:T(2,128)S(1)} %copy-done.2, ...), custom_call_target="tpu_custom_call" | custom-call | tf_op jit(solution)/shard_map/pallas_call | solution.py:344
  102.5 0.6 copy.24
  103.1 2.1 %fusion = f32[2,1024,256]{2,1,0:T(8,128)} fusion(bf16[2,320,1024]{2,1,0:T(8,128)(2,1)S(1)} %get-tuple-element.6, bf16[2,320,256]{2,1,0:T(8,128)(2,1)S(1)} %get-tuple-element.7), kind=kOutput, calls=%fused_computation.4 | convolution fusion | flops 335544320 | bytes 3735552 | tf_op jit(solution)/shard_map/lrd,lrf->ldf/dot_general | solution.py:396
  (7 shorter events, 0.2 us)
Async XLA Ops:
  0.6 4.1 %copy-start = (bf16[3,256,1024]{2,1,0:T(8,128)(2,1)S(1)}, bf16[3,256,1024]{2,1,0:T(8,128)(2,1)}, u32[]{:S(2)}) copy-start(bf16[3,256,1024]{2,1,0:T(8,128)(2,1)} %dec_hbm.1) | copy-start | bytes 4718596
  0.6 4.1 %copy-start.2 = (f32[2,256]{1,0:T(2,128)S(1)}, f32[2,256]{1,0:T(2,128)}, u32[]{:S(2)}) copy-start(f32[2,256]{1,0:T(2,128)} %bias.1) | copy-start | bytes 6148
  4.8 1.2 %copy-start.1 = (bf16[2,1024,256]{2,1,0:T(8,128)(2,1)S(1)}, bf16[2,1024,256]{2,1,0:T(8,128)(2,1)}, u32[]{:S(2)}) copy-start(bf16[2,1024,256]{2,1,0:T(8,128)(2,1)} %enc_hbm.1) | copy-start | bytes 3145732

commit v3 on v2

--- a/solution.py
+++ b/solution.py
@@ -24,11 +24,11 @@
 
 def kernel(
     nz, nf, scale,
-    act, tgt, enc_hbm, bias, dec_hbm, mask, gate,
-    recon, a_all, pre_out,
-    enc, dec, x, xf, err_all, part, grad,
+    act, tgt, enc_hbm, bias, dec_hbm, top, pairs,
+    recon, a_hbm, pre_out,
+    a_all, enc, dec, own, goal, wide_rows, mask, gate, x, xf, err_all, part, grad,
     f_out, f_in, codes, pre_grad,
-    core_out, core_in, near_out, near_in, total, far_out, far_in,
+    core_out, core_in, near_out, near_in, total, total_rows, far_out, far_in,
     load_sem, far_s, far_r, near_s, near_r, core_s, core_r,
     f_send, f_recv, rc_s, rc_r, rn_s, rn_r, rf_s, rf_r,
 ):
@@ -38,8 +38,10 @@
     y = (lat // 2) % 2
     z = lat // 4
     nq = nz // NEAR
-    q, m = z // NEAR, z % NEAR
-    rb = act.shape[1]
+    held = (z + 2) % NEAR
+    offsets = [2 - nz // 2 + NEAR * j for j in range(nq)]
+    own_rows = act.shape[0]
+    rb = own.shape[2]
     rows, depth = a_all.shape[1:]
     chunks = depth // LANES
     latents = enc.shape[2]
@@ -51,7 +53,8 @@
 
     other_core = at(z, y, 1 - c)
     near_devices = [at(z + dz, 1 - y if dy else y, c) for dz, dy, _, _ in MESSAGES]
-    far_devices = [at(z + NEAR * j, y, c) for j in range(1, nq)]
+    far_devices = [at(z + o, y, c) for o in offsets]
+    far_blocks = [((z - o + nz) % nz) // NEAR for o in offsets]
     parts = {"all": slice(0, nq), "low": slice(0, nq // 2), "high": slice(nq // 2, nq)}
 
     def span(which):
@@ -70,8 +73,35 @@
     load_dec = pltpu.make_async_copy(dec_hbm, dec, load_sem.at[1])
     load_enc.start()
     load_dec.start()
+
+    def split(ref, t, put):
+        values = ref[...].astype(F32)
+        for k in range(chunks):
+            put[t, pl.ds(k, own_rows, stride=chunks), :] = values[:, t, k * LANES:(k + 1) * LANES]
+
     for t in range(2):
-        x[0, t, m, y, c, q] = act[t]
+        split(act, t, total_rows)
+        own[0, t] = total_rows[t].astype(BF16)
+        split(tgt, t, goal)
+    local_blocks = latents // BLOCK
+    place = feat * fb + lax.broadcasted_iota(jnp.int32, (fb, rows), 0)
+    index = lax.div(place, own_rows)
+    device = lax.rem(index, nq) * (4 * NEAR) + lax.div(index, nq)
+    picked = device * own_rows + lax.rem(place, own_rows) == lax.broadcasted_iota(jnp.int32, (fb, rows), 1)
+    picked = jnp.where(picked, 1.0, 0.0).astype(BF16)
+    across = (((1,), (1,)), ((), ()))
+    for t in range(2):
+        hits = []
+        for b in range(local_blocks):
+            same = jnp.where(top[t] == lat * local_blocks + b, 1.0, 0.0)
+            hits.append(jnp.broadcast_to(jnp.sum(same, axis=0, keepdims=True), (BLOCK, rows)))
+        hits = jnp.concatenate(hits, axis=0).astype(BF16)
+        mask[t] = lax.dot_general(picked, hits, across, preferred_element_type=F32)
+    numbers = pairs[0].astype(F32)[1:2]
+    lanes = lax.broadcasted_iota(jnp.int32, numbers.shape, 1)
+    for b in range(local_blocks):
+        value = jnp.sum(jnp.where(lanes == lat * local_blocks + b, numbers, 0.0), axis=1, keepdims=True)
+        gate[:, b * BLOCK:(b + 1) * BLOCK] = jnp.broadcast_to(value, (1, BLOCK))
     pl.semaphore_wait(barrier, len(everyone))
 
     def remote(src, dst, send, recv, device):
@@ -80,22 +110,22 @@
         )
 
     def far_copy(g, t, j):
-        ref = x.at[g, t, m, y, c, q]
-        return remote(ref, ref, far_s.at[g, t, j], far_r.at[g, t, j], far_devices[j - 1])
+        ref = x.at[g, t, z % NEAR, y, c, z // NEAR]
+        return remote(own.at[g, t], ref, far_s.at[g, t, j], far_r.at[g, t, j], far_devices[j])
 
     def far_arrival(g, t, j):
-        ref = x.at[g, t, m, y, c, (q - j + nq) % nq]
-        return remote(ref, ref, far_s.at[g, t, j], far_r.at[g, t, j], far_devices[j - 1])
+        ref = x.at[g, t, held, y, c, far_blocks[j]]
+        return remote(ref, ref, far_s.at[g, t, j], far_r.at[g, t, j], far_devices[j])
 
     def near_copy(g, t, n):
-        ref = x.at[g, t, m, y, c, span(MESSAGES[n][2])]
+        ref = x.at[g, t, held, y, c, span(MESSAGES[n][2])]
         return remote(ref, ref, near_s.at[g, t, n], near_r.at[g, t, n], near_devices[n])
 
     def arrival_ref(g, t, n, cc):
         if n == len(MESSAGES):
-            return x.at[g, t, m, y, cc]
+            return x.at[g, t, held, y, cc]
         dz, dy, which, _ = MESSAGES[n]
-        return x.at[g, t, (m - dz + NEAR) % NEAR, 1 - y if dy else y, cc, span(which)]
+        return x.at[g, t, (held - dz + NEAR) % NEAR, 1 - y if dy else y, cc, span(which)]
 
     def near_arrival(g, t, n):
         ref = arrival_ref(g, t, n, c)
@@ -106,11 +136,11 @@
         return remote(ref, ref, core_s.at[g, t, n], core_r.at[g, t, n], other_core)
 
     def gather_far(g, t):
-        for j in range(1, nq):
+        for j in range(nq):
             far_copy(g, t, j).start()
 
     def gather_near(g, t):
-        for j in range(1, nq):
+        for j in range(nq):
             far_arrival(g, t, j).wait_recv()
         for n in range(len(MESSAGES)):
             near_copy(g, t, n).start()
@@ -135,7 +165,7 @@
             out[t, :, k * LANES:(k + 1) * LANES] = xf[t, pl.ds(k, rows, stride=chunks), :].astype(BF16)
 
     def gather_sent(g, t):
-        for j in range(1, nq):
+        for j in range(nq):
             far_copy(g, t, j).wait_send()
         for n in range(len(MESSAGES)):
             near_copy(g, t, n).wait_send()
@@ -188,12 +218,12 @@
     steps = (1, -1, 2, 0)
 
     def rc_copy(t, s):
-        mm = (m + steps[s] + NEAR) % NEAR
+        mm = (held + steps[s] + NEAR) % NEAR
         return remote(core_out.at[t, mm], core_in.at[t, mm], rc_s.at[t, s], rc_r.at[t, s], other_core)
 
     def reduce_core(t):
         for s in range(NEAR):
-            mm = (m + steps[s] + NEAR) % NEAR
+            mm = (held + steps[s] + NEAR) % NEAR
             for yy in range(2):
                 core_out[t, mm, yy] = blocks(local(t, mm, yy, 1 - c)).astype(BF16)
             rc_copy(t, s).start()
@@ -203,7 +233,7 @@
 
     def rn_copy(t, n):
         dz, dy, which, slot = MESSAGES[n]
-        mm = (m + dz + NEAR) % NEAR
+        mm = (held + dz + NEAR) % NEAR
         yy = 1 - y if dy else y
         return remote(
             near_out.at[t, mm, yy, span(which)], near_in.at[t, slot, span(which)],
@@ -212,7 +242,7 @@
 
     def reduce_near(t):
         for s, messages in enumerate(((0, 1), (2, 3), (4, 5, 6, 7), (8,))):
-            mm = (m + steps[s] + NEAR) % NEAR
+            mm = (held + steps[s] + NEAR) % NEAR
             rc_copy(t, s).wait_recv()
             for yy in ((y, 1 - y) if s < 3 else (1 - y,)):
                 near_out[t, mm, yy] = with_core(t, mm, yy).astype(BF16)
@@ -220,33 +250,37 @@
                 rn_copy(t, n).start()
 
     def rf_copy(t, j):
-        return remote(far_out.at[t, j], far_in.at[t, j], rf_s.at[t, j], rf_r.at[t, j], far_devices[j - 1])
+        return remote(far_out.at[t, j], far_in.at[t, j], rf_s.at[t, j], rf_r.at[t, j], far_devices[nq - 1 - j])
 
     def reduce_far(t):
         for n in range(len(MESSAGES)):
             rn_copy(t, n).wait_recv()
-        acc = with_core(t, m, y)
+        acc = with_core(t, held, y)
         for slot in range(SLOTS):
             acc = acc + near_in[t, slot].astype(F32)
         total[t] = acc
-        for j in range(1, nq):
-            far_out[t, j] = total[t, (q + j) % nq].astype(BF16)
+        for j in range(nq):
+            far_out[t, j] = total[t, far_blocks[j]].astype(BF16)
             rf_copy(t, j).start()
 
     def reduce_end(t):
-        acc = total[t, q]
-        for j in range(1, nq):
+        acc = jnp.zeros((rb, LANES), F32)
+        for j in range(nq):
             rf_copy(t, j).wait_recv()
             acc = acc + far_in[t, j].astype(F32)
-        recon[t] = acc.astype(BF16)
-        x[1, t, m, y, c, q] = (acc - tgt[t].astype(F32)).astype(BF16)
+        own[1, t] = (acc - goal[t]).astype(BF16)
+        total_rows[t] = acc
+
+    def write_recon(t):
+        for k in range(chunks):
+            wide_rows[:, t, k * LANES:(k + 1) * LANES] = total_rows[t, pl.ds(k, own_rows, stride=chunks), :]
 
     def reduce_sent(t):
         for s in range(NEAR):
             rc_copy(t, s).wait_send()
         for n in range(len(MESSAGES)):
             rn_copy(t, n).wait_send()
-        for j in range(1, nq):
+        for j in range(nq):
             rf_copy(t, j).wait_send()
 
     both = (0, 1)
@@ -257,11 +291,12 @@
     load_enc.wait()
     for t in both:
         gather_core(0, t)
-    for t in both:
         gather_end(0, t, a_all)
         part[t] = jnp.dot(a_all[t], enc[t], preferred_element_type=F32)
         sum_start(0, t, part)
-    for t in both:
+    store_act = [pltpu.make_async_copy(a_all.at[t], a_hbm.at[t], load_sem.at[2 + t]) for t in both]
+    for t in both:
+        store_act[t].start()
         codes[t, feat] = (mask[t] * (sum_end(0, t, part) + bias[t:t + 1, :])).astype(BF16)
         share_start(0, t, codes)
     load_dec.wait()
@@ -296,11 +331,12 @@
         gather_near(1, t)
     for t in both:
         reduce_sent(t)
-    for t in both:
-        gather_core(1, t)
-    across = (((1,), (1,)), ((), ()))
+        write_recon(t)
+    recon[...] = wide_rows[...].astype(BF16)
+    gather_core(1, 0)
     gather_end(1, 0, err_all)
     grad[0] = lax.dot_general(err_all[0], dec[0], across, preferred_element_type=F32)
+    gather_core(1, 1)
     gather_end(1, 1, err_all)
     grad[1] = lax.dot_general(err_all[1], dec[2], across, preferred_element_type=F32)
     sum_start(1, 1, grad)
@@ -316,6 +352,7 @@
         pre_out[t] = pre_grad[t].astype(F32).reshape(rows, latents).astype(BF16)
     for t in both:
         feature_sent(1, t, pre_grad)
+        store_act[t].wait()
 
 
 def body(nz, nf, activations, targets, enc_weight, enc_bias, dec_weight, top_blocks, pair_mask):
@@ -327,32 +364,29 @@
     rb = own_rows * chunks
     fb = rows // nf
     nq = nz // NEAR
-    first_block = lax.axis_index("latent") * local_blocks
-    feat = lax.axis_index("feature")
-    block_ids = first_block + jnp.arange(local_blocks, dtype=jnp.int32)
-    top = top_blocks.reshape(nq, NEAR, 2, 2, own_rows, layers, -1).transpose(5, 1, 2, 3, 0, 4, 6)
-    top = lax.dynamic_slice_in_dim(top.reshape(layers, rows, -1), feat * fb, fb, 1)
-    hits = jnp.any(top[..., None] == block_ids, axis=2)
-    mask = jnp.repeat(hits.astype(F32), BLOCK, axis=-1)
-    gate = lax.dynamic_slice_in_dim(pair_mask[0, 1], first_block, local_blocks, 0)
-    gate = jnp.repeat(gate.astype(F32), BLOCK)[None]
     vmem = pl.BlockSpec(memory_space=pltpu.VMEM)
-    hbm = pl.BlockSpec(memory_space=pl.ANY)
+    hbm = pl.BlockSpec(memory_space=pltpu.HBM)
     dma = pltpu.SemaphoreType.DMA
     bf, f32 = (lambda *s: pltpu.VMEM(s, BF16)), (lambda *s: pltpu.VMEM(s, F32))
     count = len(MESSAGES)
     recon, a_all, pre_grad = pl.pallas_call(
         functools.partial(kernel, nz, nf, 1.0 / math.sqrt(rows)),
         out_shape=(
-            jax.ShapeDtypeStruct((layers, rb, LANES), BF16),
+            jax.ShapeDtypeStruct(activations.shape, BF16),
             jax.ShapeDtypeStruct((layers, rows, depth), BF16),
             jax.ShapeDtypeStruct((layers, rows, latents), BF16),
         ),
         in_specs=[vmem, vmem, hbm, vmem, hbm, vmem, vmem],
-        out_specs=(vmem, vmem, vmem),
+        out_specs=(vmem, hbm, vmem),
         scratch_shapes=[
+            bf(layers, rows, depth),
             bf(*enc_weight.shape),
             bf(*dec_weight.shape),
+            bf(2, layers, rb, LANES),
+            f32(layers, rb, LANES),
+            f32(own_rows, layers, depth),
+            f32(layers, fb, latents),
+            f32(1, latents),
             bf(2, layers, NEAR, 2, 2, nq, rb, LANES),
             f32(layers, rows * chunks, LANES),
             bf(layers, rows, depth),
@@ -367,9 +401,10 @@
             bf(layers, NEAR, 2, nq, rb, LANES),
             bf(layers, SLOTS, nq, rb, LANES),
             f32(layers, nq, rb, LANES),
+            f32(layers, rb, LANES),
             bf(layers, nq, rb, LANES),
             bf(layers, nq, rb, LANES),
-            dma((2,)),
+            dma((4,)),
             dma((2, layers, nq)),
             dma((2, layers, nq)),
             dma((2, layers, count)),
@@ -386,15 +421,13 @@
             dma((layers, nq)),
         ],
         compiler_params=pltpu.CompilerParams(
-            collective_id=0, has_side_effects=True, vmem_limit_bytes=48 * 2**20
+            collective_id=0, has_side_effects=True, vmem_limit_bytes=63 * 2**20
         ),
     )(
-        activations.transpose(1, 0, 2).reshape(layers, rb, LANES),
-        targets.transpose(1, 0, 2).reshape(layers, rb, LANES),
-        enc_weight, enc_bias, dec_weight, mask, gate,
+        activations, targets, enc_weight, enc_bias, dec_weight, top_blocks.transpose(1, 2, 0), pair_mask,
     )
     enc_grad = jnp.einsum("lrd,lrf->ldf", a_all, pre_grad, preferred_element_type=F32)
-    return recon.reshape(layers, own_rows, depth).transpose(1, 0, 2), enc_grad
+    return recon, enc_grad
 
 
 def solution(mesh):

time: 106 us -> 97.4 us (0.919)
  local copies, waits for them, and re-layouts: 5.75 us -> 0.61 us
  Pallas kernels: 96.4 us -> 92.4 us
  matrix products: 2.14 us -> 3.52 us
    pallas_call x1, Pallas kernels: 96.4 us -> 92.4 us  [body(): pl.pallas_call(functools.partial(kernel, nz, nf, 1.0 / math.sqrt(rows)),...]
    unnamed x8 -> x3, local copies, waits for them, and re-layouts: 2.83 us -> 0.61 us
    transpose x3 -> x0, local copies, waits for them, and re-layouts: 1.51 us -> none  [the longest x1 0.74 us: body(): targets.transpose(1, 0, 2).reshape(layers, rb, LANES)]
    dot_general x1, matrix products: 2.14 us -> 3.52 us  [body(): jnp.einsum('lrd,lrf->ldf', a_all, pre_grad, preferred_element_type=F32)]
where the time goes in v3:
time: 97.4 us; the launch traced here: 97.2 us
  Pallas kernels  92.4 us (95%)
  matrix products  3.52 us (4%)
    pallas_call x1, Pallas kernels, body(): pl.pallas_call(functools.partial(kernel, nz, nf, 1.0 / math.sqrt(rows)),...  92.4 us
    dot_general x1, matrix products, body(): jnp.einsum('lrd,lrf->ldf', a_all, pre_grad, preferred_element_type=F32)  3.52 us

profile of v3, /device:TPU:1, one launch (start us, length us, event | category | flops | bytes accessed | tf_op | source)
XLA Modules:
  0.0 97.2 jit_solution(14064172307998691376)
XLA Ops:
  0.6 92.4 %shard_map.86 = (bf16[5,2,1024]{2,1,0:T(2,128)(2,1)}, bf16[2,320,1024]{2,1,0:T(8,128)(2,1)}, bf16[2,320,256]{2,1,0:T(8,128)(2,1)}) custom-call(bf16[5,2,1024]{2,1,0:T(2,128)(2,1)} %act.1, bf16[5,2,1024]{2,1,0:T(2,128)(2,1)} %tgt.1, bf16[2,1024,256]{2,1,0:T(8,128)(2,1)} %enc_hbm.1, f32[2,256]{1,0:T(2,128)} %bias.1, bf16[3,256,1024]{2,1,0:T(8,128)(2,1)} %dec_hbm.1, ...), custom_call_target="tpu_custom_call" | custom-call | tf_op jit(solution)/shard_map/pallas_call | solution.py:372
  93.0 0.0 copy-start
  93.0 3.5 %fusion = f32[2,1024,256]{2,1,0:T(8,128)} fusion(bf16[2,320,1024]{2,1,0:T(8,128)(2,1)} %get-tuple-element.6, bf16[2,320,256]{2,1,0:T(8,128)(2,1)} %get-tuple-element.7), kind=kOutput, calls=%fused_computation | convolution fusion | flops 335544320 | bytes 3735552 | tf_op jit(solution)/shard_map/lrd,lrf->ldf/dot_general | solution.py:429
  96.5 0.0 copy-done
  96.5 0.6 copy.10
Async XLA Ops:
  93.0 3.5 %copy-start = (bf16[5,2,1024]{2,1,0:T(2,128)(2,1)S(1)}, bf16[5,2,1024]{2,1,0:T(2,128)(2,1)}, u32[]{:S(2)}) copy-start(bf16[5,2,1024]{2,1,0:T(2,128)(2,1)} %get-tuple-element.10) | copy-start | bytes 61444

commit v4 on v3

v4 whole, which is shorter than its diff:
```python
import functools
import math

import jax
import jax.numpy as jnp
from jax import lax
from jax.experimental import pallas as pl
from jax.experimental.pallas import tpu as pltpu
from jax.sharding import PartitionSpec as P

BLOCK = 128
LANES = 128
F32 = jnp.float32
BF16 = jnp.bfloat16
MESH = pl.DeviceIdType.MESH
NEAR = 4
MESSAGES = (
    (1, 0, "all", 0), (1, 1, "all", 1), (-1, 0, "all", 2), (-1, 1, "all", 3),
    (2, 0, "low", 4), (2, 1, "low", 5), (-2, 0, "high", 4), (-2, 1, "high", 5),
    (0, 1, "all", 6),
)
SLOTS = 7


def kernel(
    nz, nf, scale,
    act, tgt, enc_hbm, bias, dec_hbm, top, pairs,
    recon, a_hbm, pre_out,
    a_own, enc, dec, biases, own, goal, wide_rows, mask, gate, x, xf, err_own, part, grad,
    f_out, f_in, codes, pre_own, pre_all,
    near_out, near_in, total, total_rows, far_out, far_in,
    load_sem, swap_s, swap_r, far_s, far_r, near_s, near_r,
    f_send, f_recv, g_send, g_recv, rn_s, rn_r, rf_s, rf_r,
):
    feat = lax.axis_index("feature")
    lat = lax.axis_index("latent")
    c = lat % 2
    y = (lat // 2) % 2
    z = lat // 4
    nq = nz // NEAR
    held = (z + 2) % NEAR
    offsets = [2 - nz // 2 + NEAR * j for j in range(nq)]
    own_rows = act.shape[0]
    rb = own.shape[2]
    rows, depth = a_own.shape[1:]
    chunks = depth // LANES
    latents = enc.shape[3]
    fb = 2 * rows // nf
    side = feat % 2
    group = nq * rb

    def at(zz, yy, cc):
        return {"latent": (((zz + nz) % nz) * 2 + yy) * 2 + cc}

    other_core = at(z, y, 1 - c)
    near_devices = [at(z + dz, 1 - y if dy else y, c) for dz, dy, _, _ in MESSAGES]
    far_devices = [at(z + o, y, c) for o in offsets]
    far_blocks = [((z - o + nz) % nz) // NEAR for o in offsets]
    parts = {"all": slice(0, nq), "low": slice(0, nq // 2), "high": slice(nq // 2, nq)}

    def span(which):
        s = parts[which]
        return pl.ds(s.start, s.stop - s.start)

    def peer(i):
        return (feat + i) % nf

    feature_devices = [{"feature": peer(i)} for i in range(1, nf)]
    cross_devices = [{"feature": peer(i), "latent": (z * 2 + y) * 2 + 1 - c} for i in range(1, nf)]
    everyone = [other_core] + near_devices + far_devices + feature_devices + cross_devices
    barrier = pltpu.get_barrier_semaphore()
    for device in everyone:
        pl.semaphore_signal(barrier, inc=1, device_id=device, device_id_type=MESH)
    load_enc = pltpu.make_async_copy(enc_hbm, enc.at[c], load_sem.at[0])
    load_dec = pltpu.make_async_copy(dec_hbm, dec.at[c], load_sem.at[1])
    load_enc.start()
    load_dec.start()

    def split(ref, t, put):
        values = ref[...].astype(F32)
        for k in range(chunks):
            put[t, pl.ds(k, own_rows, stride=chunks), :] = values[:, t, k * LANES:(k + 1) * LANES]

    for t in range(2):
        split(act, t, total_rows)
        own[0, t] = total_rows[t].astype(BF16)
        split(tgt, t, goal)
    local_blocks = latents // BLOCK
    place = feat // 2 * fb + lax.broadcasted_iota(jnp.int32, (fb, rows * 2), 0)
    first = ((z * 2 + y) * 2 + side) * local_blocks
    index = lax.div(place, own_rows)
    device = lax.rem(index, nq) * (4 * NEAR) + lax.div(index, nq) * 2 + c
    source = device * own_rows + lax.rem(place, own_rows)
    picked = source == lax.broadcasted_iota(jnp.int32, (fb, rows * 2), 1)
    picked = jnp.where(picked, 1.0, 0.0).astype(BF16)
    across = (((1,), (1,)), ((), ()))
    for t in range(2):
        hits = []
        for b in range(local_blocks):
            same = jnp.where(top[t] == first + b, 1.0, 0.0)
            hits.append(jnp.broadcast_to(jnp.sum(same, axis=0, keepdims=True), (BLOCK, rows * 2)))
        hits = jnp.concatenate(hits, axis=0).astype(BF16)
        mask[t] = lax.dot_general(picked, hits, across, preferred_element_type=F32)
    numbers = pairs[0].astype(F32)[1:2]
    lanes = lax.broadcasted_iota(jnp.int32, numbers.shape, 1)
    for b in range(2 * local_blocks):
        chosen = lanes == (z * 2 + y) * 2 * local_blocks + b
        value = jnp.sum(jnp.where(chosen, numbers, 0.0), axis=1, keepdims=True)
        gate[:, b * BLOCK:(b + 1) * BLOCK] = jnp.broadcast_to(value, (1, BLOCK))
    biases[c] = bias[...]
    pl.semaphore_wait(barrier, len(everyone))

    def remote(src, dst, send, recv, device):
        return pltpu.make_async_remote_copy(
            src_ref=src, dst_ref=dst, send_sem=send, recv_sem=recv, device_id=device, device_id_type=MESH
        )

    swaps = [
        remote(ref, out, swap_s.at[i], swap_r.at[i], other_core)
        for i, (ref, out) in enumerate(((bias, biases.at[c]), (enc_hbm, enc.at[c]), (dec_hbm, dec.at[c])))
    ]
    swapped = [
        remote(out, out, swap_s.at[i], swap_r.at[i], other_core)
        for i, out in enumerate((biases.at[1 - c], enc.at[1 - c], dec.at[1 - c]))
    ]

    def act_copy(t):
        return remote(a_own.at[t], a_hbm.at[t, c], swap_s.at[3 + t], swap_r.at[3 + t], other_core)

    def far_copy(g, t, j):
        ref = x.at[g, t, z % NEAR, y, z // NEAR]
        return remote(own.at[g, t], ref, far_s.at[g, t, j], far_r.at[g, t, j], far_devices[j])

    def far_arrival(g, t, j):
        ref = x.at[g, t, held, y, far_blocks[j]]
        return remote(ref, ref, far_s.at[g, t, j], far_r.at[g, t, j], far_devices[j])

    def near_copy(g, t, n):
        ref = x.at[g, t, held, y, span(MESSAGES[n][2])]
        return remote(ref, ref, near_s.at[g, t, n], near_r.at[g, t, n], near_devices[n])

    def near_arrival(g, t, n):
        dz, dy, which, _ = MESSAGES[n]
        ref = x.at[g, t, (held - dz + NEAR) % NEAR, 1 - y if dy else y, span(which)]
        return remote(ref, ref, near_s.at[g, t, n], near_r.at[g, t, n], near_devices[n])

    def gather_far(g, t):
        for j in range(nq):
            far_copy(g, t, j).start()

    def gather_near(g, t):
        for j in range(nq):
            far_arrival(g, t, j).wait_recv()
        for n in range(len(MESSAGES)):
            near_copy(g, t, n).start()

    def gather_end(g, t, out):
        for n in range(len(MESSAGES)):
            near_arrival(g, t, n).wait_recv()

        def widen(i, carry):
            blocks = x[g, t, i // 2, i % 2].astype(F32)
            xf[t, pl.ds(pl.multiple_of(i * group, 8), group), :] = blocks.reshape(group, LANES)
            return carry

        lax.fori_loop(0, 2 * NEAR, widen, 0)
        for k in range(chunks):
            out[t, :, k * LANES:(k + 1) * LANES] = xf[t, pl.ds(k, rows, stride=chunks), :].astype(BF16)

    def gather_sent(g, t):
        for j in range(nq):
            far_copy(g, t, j).wait_send()
        for n in range(len(MESSAGES)):
            near_copy(g, t, n).wait_send()

    def sum_copy(g, t, i):
        j = peer(i)
        return remote(
            f_out.at[g, t, j], f_in.at[g, t, i], f_send.at[0, g, t, i], f_recv.at[0, g, t, i], feature_devices[i - 1]
        )

    def sum_start(g, t, values):
        for j in range(nf):
            f_out[g, t, j] = values[t, j % 2, j // 2 * fb:(j // 2 + 1) * fb, :].astype(BF16)
        for i in range(1, nf):
            sum_copy(g, t, i).start()

    def sum_end(g, t, values):
        acc = values[t, side, pl.ds(pl.multiple_of(feat // 2 * fb, 8), fb), :]
        for i in range(1, nf):
            sum_copy(g, t, i).wait_recv()
            acc = acc + f_in[g, t, i].astype(F32)
        return acc

    def share_copy(t, i, mine):
        slot = codes.at[t, feat if mine else (feat - i + nf) % nf]
        return remote(slot, slot, f_send.at[1, 0, t, i], f_recv.at[1, 0, t, i], feature_devices[i - 1])

    def share_start(t):
        for i in range(1, nf):
            share_copy(t, i, True).start()

    def share_end(t):
        for i in range(1, nf):
            share_copy(t, i, False).wait_recv()

    def give_copy(t, i):
        target = {"feature": peer(i), "latent": (z * 2 + y) * 2 + side}
        return remote(
            pre_own.at[t], pre_all.at[t, c, feat // 2], g_send.at[t, i], g_recv.at[t, c, feat // 2], target
        )

    def give_start(t):
        for i in range(1, nf):
            give_copy(t, i).start()

        @pl.when(side != c)
        def _():
            give_copy(t, 0).start()

        @pl.when(side == c)
        def _():
            pre_all[t, c, feat // 2] = pre_own[t]

    def give_end(t):
        for k in range(nf // 2):
            for cc in range(2):
                slot = pre_all.at[t, cc, k]
                arrival = remote(slot, slot, g_send.at[t, 0], g_recv.at[t, cc, k], other_core)

                @pl.when(jnp.logical_not((cc == c) & (2 * k + c == feat)))
                def _():
                    arrival.wait_recv()

    def give_sent(t):
        for i in range(1, nf):
            give_copy(t, i).wait_send()

        @pl.when(side != c)
        def _():
            give_copy(t, 0).wait_send()

    def sum_sent(g, t):
        for i in range(1, nf):
            sum_copy(g, t, i).wait_send()

    def local(t, mm, yy):
        start = (mm * 2 + yy) * group
        return blocks(xf[t, pl.ds(pl.multiple_of(start, 8), group), :])

    def blocks(value):
        return value.reshape(nq, rb, LANES)

    steps = (1, -1, 2, 0)

    def rn_copy(t, n):
        dz, dy, which, slot = MESSAGES[n]
        mm = (held + dz + NEAR) % NEAR
        yy = 1 - y if dy else y
        return remote(
            near_out.at[t, mm, yy, span(which)], near_in.at[t, slot, span(which)],
            rn_s.at[t, n], rn_r.at[t, n], near_devices[n],
        )

    def reduce_near(t):
        for s, messages in enumerate(((0, 1), (2, 3), (4, 5, 6, 7), (8,))):
            mm = (held + steps[s] + NEAR) % NEAR
            for yy in ((y, 1 - y) if s < 3 else (1 - y,)):
                near_out[t, mm, yy] = local(t, mm, yy).astype(BF16)
            for n in messages:
                rn_copy(t, n).start()

    def rf_copy(t, j):
        return remote(far_out.at[t, j], far_in.at[t, j], rf_s.at[t, j], rf_r.at[t, j], far_devices[nq - 1 - j])

    def reduce_far(t):
        for n in range(len(MESSAGES)):
            rn_copy(t, n).wait_recv()
        acc = local(t, held, y)
        for slot in range(SLOTS):
            acc = acc + near_in[t, slot].astype(F32)
        total[t] = acc
        for j in range(nq):
            far_out[t, j] = total[t, far_blocks[j]].astype(BF16)
            rf_copy(t, j).start()

    def reduce_end(t):
        acc = jnp.zeros((rb, LANES), F32)
        for j in range(nq):
            rf_copy(t, j).wait_recv()
            acc = acc + far_in[t, j].astype(F32)
        own[1, t] = (acc - goal[t]).astype(BF16)
        total_rows[t] = acc

    def write_recon(t):
        for k in range(chunks):
            wide_rows[:, t, k * LANES:(k + 1) * LANES] = total_rows[t, pl.ds(k, own_rows, stride=chunks), :]

    def reduce_sent(t):
        for n in range(len(MESSAGES)):
            rn_copy(t, n).wait_send()
        for j in range(nq):
            rf_copy(t, j).wait_send()

    both = (0, 1)
    for t in both:
        gather_far(0, t)
    for copy in swaps:
        copy.start()
    for t in both:
        gather_near(0, t)
    load_enc.wait()
    for copy in swapped[:2]:
        copy.wait_recv()
    for t in both:
        gather_end(0, t, a_own)
        for cc in range(2):
            part[t, cc] = jnp.dot(a_own[t], enc[cc, t], preferred_element_type=F32)
        sum_start(0, t, part)
    store_act = [pltpu.make_async_copy(a_own.at[t], a_hbm.at[t, c], load_sem.at[2 + t]) for t in both]
    for t in both:
        store_act[t].start()
        act_copy(t).start()
        value = sum_end(0, t, part) + biases[side, t:t + 1, :]
        codes[t, feat] = (mask[t] * value).astype(BF16)
        share_start(t)
    load_dec.wait()
    swapped[2].wait_recv()

    def whole(t, cc):
        mine = [codes[t, 2 * k + cc].astype(F32) for k in range(nf // 2)]
        return jnp.concatenate(mine, axis=0)

    wide = 2 * LANES
    for t in both:
        share_end(t)
        terms = []
        for cc in range(2):
            if t == 0:
                terms.append((whole(0, cc).astype(BF16), cc, 0))
            else:
                lanes = slice(cc * latents, (cc + 1) * latents)
                terms.append(((whole(0, cc) * gate[:, lanes]).astype(BF16), cc, 1))
                terms.append((whole(1, cc).astype(BF16), cc, 2))
        for n in range(depth // wide):
            cols = slice(n * wide, (n + 1) * wide)
            value = sum(jnp.dot(code, dec[cc, p, :, cols], preferred_element_type=F32) for code, cc, p in terms)
            for k in range(2):
                xf[t, pl.ds(2 * n + k, rows, stride=chunks), :] = value[:, k * LANES:(k + 1) * LANES]
        reduce_near(t)
    for copy in swaps:
        copy.wait_send()
    for t in both:
        gather_sent(0, t)
        sum_sent(0, t)
        for i in range(1, nf):
            share_copy(t, i, True).wait_send()
    for t in both:
        reduce_far(t)
    for t in both:
        reduce_end(t)
        gather_far(1, t)
    for t in both:
        gather_near(1, t)
    for t in both:
        reduce_sent(t)
        write_recon(t)
    recon[...] = wide_rows[...].astype(BF16)

    def gradient(t, cc, p):
        return lax.dot_general(err_own[t], dec[cc, p], across, preferred_element_type=F32)

    gather_end(1, 0, err_own)
    for cc in range(2):
        grad[0, cc] = gradient(0, cc, 0)
    gather_end(1, 1, err_own)
    for cc in range(2):
        grad[1, cc] = gradient(1, cc, 2)
    sum_start(1, 1, grad)
    for cc in range(2):
        grad[0, cc] = grad[0, cc] + gate[:, cc * latents:(cc + 1) * latents] * gradient(1, cc, 1)
    sum_start(1, 0, grad)
    for t in (1, 0):
        pre_own[t] = (mask[t] * sum_end(1, t, grad) * scale).astype(BF16)
        give_start(t)
    for t in both:
        gather_sent(1, t)
        sum_sent(1, t)
        store_act[t].wait()
        act_copy(t).wait_send()
        arrived = a_hbm.at[t, 1 - c]
        remote(arrived, arrived, swap_s.at[3 + t], swap_r.at[3 + t], other_core).wait_recv()
    for t in (1, 0):
        give_end(t)
        for cc in range(2):
            whole_rows = jnp.concatenate([pre_all[t, cc, k].astype(F32) for k in range(nf // 2)], axis=0)
            pre_out[t, cc] = whole_rows.astype(BF16)
    for t in both:
        give_sent(t)


def body(nz, nf, activations, targets, enc_weight, enc_bias, dec_weight, top_blocks, pair_mask):
    own_rows, layers, depth = activations.shape
    all_rows = top_blocks.shape[0]
    rows = all_rows // 2
    latents = enc_weight.shape[2]
    chunks = depth // LANES
    rb = own_rows * chunks
    fb = all_rows // nf
    nq = nz // NEAR
    vmem = pl.BlockSpec(memory_space=pltpu.VMEM)
    hbm = pl.BlockSpec(memory_space=pltpu.HBM)
    dma = pltpu.SemaphoreType.DMA
    bf, f32 = (lambda *s: pltpu.VMEM(s, BF16)), (lambda *s: pltpu.VMEM(s, F32))
    count = len(MESSAGES)
    recon, a_all, pre_grad = pl.pallas_call(
        functools.partial(kernel, nz, nf, 1.0 / math.sqrt(all_rows)),
        out_shape=(
            jax.ShapeDtypeStruct(activations.shape, BF16),
            jax.ShapeDtypeStruct((layers, 2, rows, depth), BF16),
            jax.ShapeDtypeStruct((layers, 2, rows, latents), BF16),
        ),
        in_specs=[vmem, vmem, hbm, vmem, hbm, vmem, vmem],
        out_specs=(vmem, hbm, vmem),
        scratch_shapes=[
            bf(layers, rows, depth),
            bf(2, *enc_weight.shape),
            bf(2, *dec_weight.shape),
            f32(2, *enc_bias.shape),
            bf(2, layers, rb, LANES),
            f32(layers, rb, LANES),
            f32(own_rows, layers, depth),
            f32(layers, fb, latents),
            f32(1, 2 * latents),
            bf(2, layers, NEAR, 2, nq, rb, LANES),
            f32(layers, rows * chunks, LANES),
            bf(layers, rows, depth),
            f32(layers, 2, rows, latents),
            f32(layers, 2, rows, latents),
            bf(2, layers, nf, fb, latents),
            bf(2, layers, nf, fb, latents),
            bf(layers, nf, fb, latents),
            bf(layers, fb, latents),
            bf(layers, 2, nf // 2, fb, latents),
            bf(layers, NEAR, 2, nq, rb, LANES),
            bf(layers, SLOTS, nq, rb, LANES),
            f32(layers, nq, rb, LANES),
            f32(layers, rb, LANES),
            bf(layers, nq, rb, LANES),
            bf(layers, nq, rb, LANES),
            dma((4,)),
            dma((5,)),
            dma((5,)),
            dma((2, layers, nq)),
            dma((2, layers, nq)),
            dma((2, layers, count)),
            dma((2, layers, count)),
            dma((2, 2, layers, nf)),
            dma((2, 2, layers, nf)),
            dma((layers, nf)),
            dma((layers, 2, nf // 2)),
            dma((layers, count)),
            dma((layers, count)),
            dma((layers, nq)),
            dma((layers, nq)),
        ],
        compiler_params=pltpu.CompilerParams(
            collective_id=0, has_side_effects=True, vmem_limit_bytes=63 * 2**20
        ),
    )(
        activations, targets, enc_weight, enc_bias, dec_weight, top_blocks.transpose(1, 2, 0), pair_mask,
    )
    enc_grad = jnp.einsum(
        "lrd,lrf->ldf",
        a_all.reshape(layers, all_rows, depth),
        pre_grad.reshape(layers, all_rows, latents),
        preferred_element_type=F32,
    )
    return recon, enc_grad


def solution(mesh):
    in_specs = (
        P("latent", None, "feature"),
        P("latent", None, "feature"),
        P(None, "feature", "latent"),
        P(None, "latent"),
        P(None, "latent", "feature"),
        P(),
        P(),
    )
    out_specs = (P("latent", None, "feature"), P(None, "feature", "latent"))
    step = functools.partial(body, mesh.shape["latent"] // 4, mesh.shape["feature"])
    return jax.shard_map(step, mesh=mesh, in_specs=in_specs, out_specs=out_specs, check_vma=False)
```

time: 97.4 us -> 92.2 us (0.947)
  Pallas kernels: 92.4 us -> 87.2 us
    pallas_call x1, Pallas kernels: 92.4 us -> 87.2 us  [body(): pl.pallas_call(functools.partial(kernel, nz, nf, 1.0 / math.sqrt(all_rows...]
where the time goes in v4:
time: 92.2 us; the launch traced here: 92 us
  Pallas kernels  87.2 us (95%)
  matrix products  3.52 us (4%)
    pallas_call x1, Pallas kernels, body(): pl.pallas_call(functools.partial(kernel, nz, nf, 1.0 / math.sqrt(all_rows...  87.2 us
    dot_general x1, matrix products, body(): jnp.einsum('lrd,lrf->ldf', a_all.reshape(layers, all_rows, depth), pre_gr...  3.52 us

profile of v4, /device:TPU:1, one launch (start us, length us, event | category | flops | bytes accessed | tf_op | source)
XLA Modules:
  0.0 92.0 jit_solution(2212379285076264644)
XLA Ops:
  0.6 87.2 %shard_map.86 = (bf16[5,2,1024]{2,1,0:T(2,128)(2,1)}, bf16[2,2,160,1024]{3,2,1,0:T(8,128)(2,1)}, bf16[2,2,160,256]{3,2,1,0:T(8,128)(2,1)}) custom-call(bf16[5,2,1024]{2,1,0:T(2,128)(2,1)} %act.1, bf16[5,2,1024]{2,1,0:T(2,128)(2,1)} %tgt.1, bf16[2,1024,256]{2,1,0:T(8,128)(2,1)} %enc_hbm.1, f32[2,256]{1,0:T(2,128)} %bias.1, bf16[3,256,1024]{2,1,0:T(8,128)(2,1)} %dec_hbm.1, ...), custom_call_target="tpu_custom_call" | custom-call | tf_op jit(solution)/shard_map/pallas_call | solution.py:416
  87.8 0.0 copy-start
  87.9 3.5 %fusion = f32[2,1024,256]{2,1,0:T(8,128)} fusion(bf16[2,320,1024]{2,1,0:T(8,128)(2,1)} %bitcast.5, bf16[2,320,256]{2,1,0:T(8,128)(2,1)} %bitcast.6), kind=kOutput, calls=%fused_computation | convolution fusion | flops 335544320 | bytes 3735552 | tf_op jit(solution)/shard_map/lrd,lrf->ldf/dot_general | solution.py:473
  91.4 0.0 copy-done
  91.4 0.6 copy.10
Async XLA Ops:
  87.8 3.5 %copy-start = (bf16[5,2,1024]{2,1,0:T(2,128)(2,1)S(1)}, bf16[5,2,1024]{2,1,0:T(2,128)(2,1)}, u32[]{:S(2)}) copy-start(bf16[5,2,1024]{2,1,0:T(2,128)(2,1)} %get-tuple-element.10) | copy-start | bytes 61444

commit v5 on v4

--- a/solution.py
+++ b/solution.py
@@ -15,21 +15,21 @@
 MESH = pl.DeviceIdType.MESH
 NEAR = 4
 MESSAGES = (
-    (1, 0, "all", 0), (1, 1, "all", 1), (-1, 0, "all", 2), (-1, 1, "all", 3),
-    (2, 0, "low", 4), (2, 1, "low", 5), (-2, 0, "high", 4), (-2, 1, "high", 5),
-    (0, 1, "all", 6),
+    (2, 1, "low", 5), (-2, 1, "high", 5), (1, 1, "all", 1), (-1, 1, "all", 3),
+    (2, 0, "low", 4), (-2, 0, "high", 4), (0, 1, "all", 6), (1, 0, "all", 0), (-1, 0, "all", 2),
 )
+ARRIVALS = (7, 8, 4, 5, 6, 2, 3, 0, 1)
 SLOTS = 7
 
 
 def kernel(
     nz, nf, scale,
-    act, tgt, enc_hbm, bias, dec_hbm, top, pairs,
-    recon, a_hbm, pre_out,
-    a_own, enc, dec, biases, own, goal, wide_rows, mask, gate, x, xf, err_own, part, grad,
+    act_hbm, tgt_hbm, enc_hbm, bias_hbm, dec_hbm, top_hbm, pairs_hbm,
+    recon_hbm, a_hbm, pre_hbm,
+    act, tgt, bias, top, pairs, recon, pre_out, a_own, enc, dec, biases, own, goal, wide_rows, mask, gate, x, xf, err_own, part, grad,
     f_out, f_in, codes, pre_own, pre_all,
     near_out, near_in, total, total_rows, far_out, far_in,
-    load_sem, swap_s, swap_r, far_s, far_r, near_s, near_r,
+    load_sem, small_sem, swap_s, swap_r, far_s, far_r, near_s, near_r,
     f_send, f_recv, g_send, g_recv, rn_s, rn_r, rf_s, rf_r,
 ):
     feat = lax.axis_index("feature")
@@ -41,6 +41,8 @@
     held = (z + 2) % NEAR
     offsets = [2 - nz // 2 + NEAR * j for j in range(nq)]
     own_rows = act.shape[0]
+    inputs = ((act_hbm, act), (tgt_hbm, tgt), (bias_hbm, bias), (top_hbm, top), (pairs_hbm, pairs))
+    loads = [pltpu.make_async_copy(a, b, small_sem.at[i]) for i, (a, b) in enumerate(inputs)]
     rb = own.shape[2]
     rows, depth = a_own.shape[1:]
     chunks = depth // LANES
@@ -62,8 +64,15 @@
         s = parts[which]
         return pl.ds(s.start, s.stop - s.start)
 
+    relations = [(0, 0)] + [(a, b) for a, b in ((1, 2), (0, 2), (1, 1), (1, 3), (0, 1), (0, 3), (1, 0))]
+
     def peer(i):
-        return (feat + i) % nf
+        a, b = relations[i]
+        return (feat // 4 + a) % 2 * 4 + (feat % 4 + b) % 4
+
+    def giver(i):
+        a, b = relations[i]
+        return (feat // 4 + a) % 2 * 4 + (feat % 4 + 4 - b) % 4
 
     feature_devices = [{"feature": peer(i)} for i in range(1, nf)]
     cross_devices = [{"feature": peer(i), "latent": (z * 2 + y) * 2 + 1 - c} for i in range(1, nf)]
@@ -71,10 +80,15 @@
     barrier = pltpu.get_barrier_semaphore()
     for device in everyone:
         pl.semaphore_signal(barrier, inc=1, device_id=device, device_id_type=MESH)
+    for copy in loads:
+        copy.start()
     load_enc = pltpu.make_async_copy(enc_hbm, enc.at[c], load_sem.at[0])
     load_dec = pltpu.make_async_copy(dec_hbm, dec.at[c], load_sem.at[1])
     load_enc.start()
     load_dec.start()
+
+    for copy in loads:
+        copy.wait()
 
     def split(ref, t, put):
         values = ref[...].astype(F32)
@@ -155,15 +169,18 @@
             near_copy(g, t, n).start()
 
     def gather_end(g, t, out):
-        for n in range(len(MESSAGES)):
+        def widen(mm, yy, which):
+            piece = parts[which]
+            count = (piece.stop - piece.start) * rb
+            start = ((mm * 2 + yy) * nq + piece.start) * rb
+            values = x[g, t, mm, yy, span(which)].astype(F32).reshape(count, LANES)
+            xf[t, pl.ds(pl.multiple_of(start, 8), count), :] = values
+
+        widen(held, y, "all")
+        for n in ARRIVALS:
+            dz, dy, which, _ = MESSAGES[n]
             near_arrival(g, t, n).wait_recv()
-
-        def widen(i, carry):
-            blocks = x[g, t, i // 2, i % 2].astype(F32)
-            xf[t, pl.ds(pl.multiple_of(i * group, 8), group), :] = blocks.reshape(group, LANES)
-            return carry
-
-        lax.fori_loop(0, 2 * NEAR, widen, 0)
+            widen((held - dz + NEAR) % NEAR, 1 - y if dy else y, which)
         for k in range(chunks):
             out[t, :, k * LANES:(k + 1) * LANES] = xf[t, pl.ds(k, rows, stride=chunks), :].astype(BF16)
 
@@ -193,7 +210,7 @@
         return acc
 
     def share_copy(t, i, mine):
-        slot = codes.at[t, feat if mine else (feat - i + nf) % nf]
+        slot = codes.at[t, feat if mine else giver(i)]
         return remote(slot, slot, f_send.at[1, 0, t, i], f_recv.at[1, 0, t, i], feature_devices[i - 1])
 
     def share_start(t):
@@ -250,8 +267,6 @@
 
     def blocks(value):
         return value.reshape(nq, rb, LANES)
-
-    steps = (1, -1, 2, 0)
 
     def rn_copy(t, n):
         dz, dy, which, slot = MESSAGES[n]
@@ -263,12 +278,12 @@
         )
 
     def reduce_near(t):
-        for s, messages in enumerate(((0, 1), (2, 3), (4, 5, 6, 7), (8,))):
-            mm = (held + steps[s] + NEAR) % NEAR
-            for yy in ((y, 1 - y) if s < 3 else (1 - y,)):
+        for n, (dz, dy, which, _) in enumerate(MESSAGES):
+            if which != "high":
+                mm = (held + dz + NEAR) % NEAR
+                yy = 1 - y if dy else y
                 near_out[t, mm, yy] = local(t, mm, yy).astype(BF16)
-            for n in messages:
-                rn_copy(t, n).start()
+            rn_copy(t, n).start()
 
     def rf_copy(t, j):
         return remote(far_out.at[t, j], far_in.at[t, j], rf_s.at[t, j], rf_r.at[t, j], far_devices[nq - 1 - j])
@@ -366,6 +381,8 @@
         reduce_sent(t)
         write_recon(t)
     recon[...] = wide_rows[...].astype(BF16)
+    store_recon = pltpu.make_async_copy(recon, recon_hbm, small_sem.at[0])
+    store_recon.start()
 
     def gradient(t, cc, p):
         return lax.dot_general(err_own[t], dec[cc, p], across, preferred_element_type=F32)
@@ -390,13 +407,17 @@
         act_copy(t).wait_send()
         arrived = a_hbm.at[t, 1 - c]
         remote(arrived, arrived, swap_s.at[3 + t], swap_r.at[3 + t], other_core).wait_recv()
+    store_pre = [pltpu.make_async_copy(pre_out.at[t], pre_hbm.at[t], small_sem.at[1 + t]) for t in both]
     for t in (1, 0):
         give_end(t)
         for cc in range(2):
             whole_rows = jnp.concatenate([pre_all[t, cc, k].astype(F32) for k in range(nf // 2)], axis=0)
             pre_out[t, cc] = whole_rows.astype(BF16)
+        store_pre[t].start()
+    store_recon.wait()
     for t in both:
         give_sent(t)
+        store_pre[t].wait()
 
 
 def body(nz, nf, activations, targets, enc_weight, enc_bias, dec_weight, top_blocks, pair_mask):
@@ -408,7 +429,6 @@
     rb = own_rows * chunks
     fb = all_rows // nf
     nq = nz // NEAR
-    vmem = pl.BlockSpec(memory_space=pltpu.VMEM)
     hbm = pl.BlockSpec(memory_space=pltpu.HBM)
     dma = pltpu.SemaphoreType.DMA
     bf, f32 = (lambda *s: pltpu.VMEM(s, BF16)), (lambda *s: pltpu.VMEM(s, F32))
@@ -420,9 +440,16 @@
             jax.ShapeDtypeStruct((layers, 2, rows, depth), BF16),
             jax.ShapeDtypeStruct((layers, 2, rows, latents), BF16),
         ),
-        in_specs=[vmem, vmem, hbm, vmem, hbm, vmem, vmem],
-        out_specs=(vmem, hbm, vmem),
+        in_specs=[hbm] * 7,
+        out_specs=(hbm, hbm, hbm),
         scratch_shapes=[
+            bf(*activations.shape),
+            bf(*targets.shape),
+            f32(*enc_bias.shape),
+            pltpu.VMEM((layers, top_blocks.shape[2], all_rows), jnp.int32),
+            pltpu.VMEM(pair_mask.shape, jnp.int32),
+            bf(*activations.shape),
+            bf(layers, 2, rows, latents),
             bf(layers, rows, depth),
             bf(2, *enc_weight.shape),
             bf(2, *dec_weight.shape),
@@ -451,6 +478,7 @@
             dma((4,)),
             dma((5,)),
             dma((5,)),
+            dma((5,)),
             dma((2, layers, nq)),
             dma((2, layers, nq)),
             dma((2, layers, count)),

time: 92.2 us -> 89 us (0.965)
  Pallas kernels: 87.2 us -> 84 us
    pallas_call x1, Pallas kernels: 87.2 us -> 84 us  [body(): pl.pallas_call(functools.partial(kernel, nz, nf, 1.0 / math.sqrt(all_rows...]
where the time goes in v5:
time: 89 us; the launch traced here: 88.8 us
  Pallas kernels  84 us (94%)
  matrix products  3.52 us (4%)
    pallas_call x1, Pallas kernels, body(): pl.pallas_call(functools.partial(kernel, nz, nf, 1.0 / math.sqrt(all_rows...  84 us
    dot_general x1, matrix products, body(): jnp.einsum('lrd,lrf->ldf', a_all.reshape(layers, all_rows, depth), pre_gr...  3.52 us

profile of v5, /device:TPU:1, one launch (start us, length us, event | category | flops | bytes accessed | tf_op | source)
XLA Modules:
  0.0 88.8 jit_solution(9746550557290039417)
XLA Ops:
  0.6 84.0 %shard_map.86 = (bf16[5,2,1024]{2,1,0:T(2,128)(2,1)}, bf16[2,2,160,1024]{3,2,1,0:T(8,128)(2,1)}, bf16[2,2,160,256]{3,2,1,0:T(8,128)(2,1)}) custom-call(bf16[5,2,1024]{2,1,0:T(2,128)(2,1)} %act_hbm.1, bf16[5,2,1024]{2,1,0:T(2,128)(2,1)} %tgt_hbm.1, bf16[2,1024,256]{2,1,0:T(8,128)(2,1)} %enc_hbm.1, f32[2,256]{1,0:T(2,128)} %bias_hbm.1, ...), custom_call_target="tpu_custom_call" | custom-call | tf_op jit(solution)/shard_map/pallas_call | solution.py:436
  84.7 0.0 copy-start
  84.7 3.5 %fusion = f32[2,1024,256]{2,1,0:T(8,128)} fusion(bf16[2,320,1024]{2,1,0:T(8,128)(2,1)} %bitcast.5, bf16[2,320,256]{2,1,0:T(8,128)(2,1)} %bitcast.6), kind=kOutput, calls=%fused_computation | convolution fusion | flops 335544320 | bytes 3735552 | tf_op jit(solution)/shard_map/lrd,lrf->ldf/dot_general | solution.py:501
  88.2 0.0 copy-done
  88.2 0.6 copy.10
Async XLA Ops:
  84.7 3.5 %copy-start = (bf16[5,2,1024]{2,1,0:T(2,128)(2,1)S(1)}, bf16[5,2,1024]{2,1,0:T(2,128)(2,1)}, u32[]{:S(2)}) copy-start(bf16[5,2,1024]{2,1,0:T(2,128)(2,1)} %get-tuple-element.10) | copy-start | bytes 61444

commit v6 on v5

--- a/solution.py
+++ b/solution.py
@@ -57,6 +57,7 @@
     other_core = at(z, y, 1 - c)
     near_devices = [at(z + dz, 1 - y if dy else y, c) for dz, dy, _, _ in MESSAGES]
     far_devices = [at(z + o, y, c) for o in offsets]
+    far_order = sorted(range(nq), key=lambda j: -abs(offsets[j]))
     far_blocks = [((z - o + nz) % nz) // NEAR for o in offsets]
     parts = {"all": slice(0, nq), "low": slice(0, nq // 2), "high": slice(nq // 2, nq)}
 
@@ -76,7 +77,7 @@
 
     feature_devices = [{"feature": peer(i)} for i in range(1, nf)]
     cross_devices = [{"feature": peer(i), "latent": (z * 2 + y) * 2 + 1 - c} for i in range(1, nf)]
-    everyone = [other_core] + near_devices + far_devices + feature_devices + cross_devices
+    everyone = [far_devices[j] for j in far_order] + cross_devices + feature_devices + near_devices + [other_core]
     barrier = pltpu.get_barrier_semaphore()
     for device in everyone:
         pl.semaphore_signal(barrier, inc=1, device_id=device, device_id_type=MESH)
@@ -159,7 +160,7 @@
         return remote(ref, ref, near_s.at[g, t, n], near_r.at[g, t, n], near_devices[n])
 
     def gather_far(g, t):
-        for j in range(nq):
+        for j in far_order:
             far_copy(g, t, j).start()
 
     def gather_near(g, t):
@@ -197,9 +198,10 @@
         )
 
     def sum_start(g, t, values):
-        for j in range(nf):
-            f_out[g, t, j] = values[t, j % 2, j // 2 * fb:(j // 2 + 1) * fb, :].astype(BF16)
-        for i in range(1, nf):
+        for i in range(1, nf):
+            j = peer(i)
+            start = pl.multiple_of(j // 2 * fb, 8)
+            f_out[g, t, j] = values[t, j % 2, pl.ds(start, fb), :].astype(BF16)
             sum_copy(g, t, i).start()
 
     def sum_end(g, t, values):
@@ -289,19 +291,18 @@
         return remote(far_out.at[t, j], far_in.at[t, j], rf_s.at[t, j], rf_r.at[t, j], far_devices[nq - 1 - j])
 
     def reduce_far(t):
-        for n in range(len(MESSAGES)):
+        total[t] = local(t, held, y)
+        for n in ARRIVALS:
+            _, _, which, slot = MESSAGES[n]
             rn_copy(t, n).wait_recv()
-        acc = local(t, held, y)
-        for slot in range(SLOTS):
-            acc = acc + near_in[t, slot].astype(F32)
-        total[t] = acc
-        for j in range(nq):
+            total[t, span(which)] = total[t, span(which)] + near_in[t, slot, span(which)].astype(F32)
+        for j in far_order:
             far_out[t, j] = total[t, far_blocks[j]].astype(BF16)
             rf_copy(t, j).start()
 
     def reduce_end(t):
         acc = jnp.zeros((rb, LANES), F32)
-        for j in range(nq):
+        for j in reversed(far_order):
             rf_copy(t, j).wait_recv()
             acc = acc + far_in[t, j].astype(F32)
         own[1, t] = (acc - goal[t]).astype(BF16)

time: 89 us -> 87.6 us (0.984)
  Pallas kernels: 84 us -> 82.7 us
    pallas_call x1, Pallas kernels: 84 us -> 82.7 us  [body(): pl.pallas_call(functools.partial(kernel, nz, nf, 1.0 / math.sqrt(all_rows...]
where the time goes in v6:
time: 87.6 us; the launch traced here: 87.5 us
  Pallas kernels  82.7 us (94%)
  matrix products  3.52 us (4%)
    pallas_call x1, Pallas kernels, body(): pl.pallas_call(functools.partial(kernel, nz, nf, 1.0 / math.sqrt(all_rows...  82.7 us
    dot_general x1, matrix products, body(): jnp.einsum('lrd,lrf->ldf', a_all.reshape(layers, all_rows, depth), pre_gr...  3.52 us

profile of v6, /device:TPU:1, one launch (start us, length us, event | category | flops | bytes accessed | tf_op | source)
XLA Modules:
  0.0 87.5 jit_solution(7218339204447341286)
XLA Ops:
  0.6 82.7 %shard_map.86 = (bf16[5,2,1024]{2,1,0:T(2,128)(2,1)}, bf16[2,2,160,1024]{3,2,1,0:T(8,128)(2,1)}, bf16[2,2,160,256]{3,2,1,0:T(8,128)(2,1)}) custom-call(bf16[5,2,1024]{2,1,0:T(2,128)(2,1)} %act_hbm.1, bf16[5,2,1024]{2,1,0:T(2,128)(2,1)} %tgt_hbm.1, bf16[2,1024,256]{2,1,0:T(8,128)(2,1)} %enc_hbm.1, f32[2,256]{1,0:T(2,128)} %bias_hbm.1, ...), custom_call_target="tpu_custom_call" | custom-call | tf_op jit(solution)/shard_map/pallas_call | solution.py:437
  83.3 0.0 copy-start
  83.4 3.5 %fusion = f32[2,1024,256]{2,1,0:T(8,128)} fusion(bf16[2,320,1024]{2,1,0:T(8,128)(2,1)} %bitcast.5, bf16[2,320,256]{2,1,0:T(8,128)(2,1)} %bitcast.6), kind=kOutput, calls=%fused_computation | convolution fusion | flops 335544320 | bytes 3735552 | tf_op jit(solution)/shard_map/lrd,lrf->ldf/dot_general | solution.py:502
  86.9 0.0 copy-done
  86.9 0.6 copy.10
Async XLA Ops:
  83.3 3.5 %copy-start = (bf16[5,2,1024]{2,1,0:T(2,128)(2,1)S(1)}, bf16[5,2,1024]{2,1,0:T(2,128)(2,1)}, u32[]{:S(2)}) copy-start(bf16[5,2,1024]{2,1,0:T(2,128)(2,1)} %get-tuple-element.10) | copy-start | bytes 61444

commit v7 on v6

--- a/solution.py
+++ b/solution.py
@@ -321,10 +321,10 @@
     both = (0, 1)
     for t in both:
         gather_far(0, t)
+    for t in both:
+        gather_near(0, t)
     for copy in swaps:
         copy.start()
-    for t in both:
-        gather_near(0, t)
     load_enc.wait()
     for copy in swapped[:2]:
         copy.wait_recv()

time: 87.6 us -> 88.1 us (level)
  no operation moved by 1% of the time
where the time goes in v7:
time: 88.1 us; the launch traced here: 87.9 us
  Pallas kernels  83.2 us (94%)
  matrix products  3.52 us (4%)
    pallas_call x1, Pallas kernels, body(): pl.pallas_call(functools.partial(kernel, nz, nf, 1.0 / math.sqrt(all_rows...  83.2 us
    dot_general x1, matrix products, body(): jnp.einsum('lrd,lrf->ldf', a_all.reshape(layers, all_rows, depth), pre_gr...  3.52 us

profile of v7, /device:TPU:1, one launch (start us, length us, event | category | flops | bytes accessed | tf_op | source)
XLA Modules:
  0.0 87.9 jit_solution(6329756448173672008)
XLA Ops:
  0.6 83.2 %shard_map.86 = (bf16[5,2,1024]{2,1,0:T(2,128)(2,1)}, bf16[2,2,160,1024]{3,2,1,0:T(8,128)(2,1)}, bf16[2,2,160,256]{3,2,1,0:T(8,128)(2,1)}) custom-call(bf16[5,2,1024]{2,1,0:T(2,128)(2,1)} %act_hbm.1, bf16[5,2,1024]{2,1,0:T(2,128)(2,1)} %tgt_hbm.1, bf16[2,1024,256]{2,1,0:T(8,128)(2,1)} %enc_hbm.1, f32[2,256]{1,0:T(2,128)} %bias_hbm.1, ...), custom_call_target="tpu_custom_call" | custom-call | tf_op jit(solution)/shard_map/pallas_call | solution.py:437
  83.8 0.0 copy-start
  83.8 3.5 %fusion = f32[2,1024,256]{2,1,0:T(8,128)} fusion(bf16[2,320,1024]{2,1,0:T(8,128)(2,1)} %bitcast.5, bf16[2,320,256]{2,1,0:T(8,128)(2,1)} %bitcast.6), kind=kOutput, calls=%fused_computation | convolution fusion | flops 335544320 | bytes 3735552 | tf_op jit(solution)/shard_map/lrd,lrf->ldf/dot_general | solution.py:502
  87.3 0.0 copy-done
  87.3 0.6 copy.10
Async XLA Ops:
  83.8 3.5 %copy-start = (bf16[5,2,1024]{2,1,0:T(2,128)(2,1)S(1)}, bf16[5,2,1024]{2,1,0:T(2,128)(2,1)}, u32[]{:S(2)}) copy-start(bf16[5,2,1024]{2,1,0:T(2,128)(2,1)} %get-tuple-element.10) | copy-start | bytes 61444

commit v8 on v6

--- a/solution.py
+++ b/solution.py
@@ -206,7 +206,7 @@
 
     def sum_end(g, t, values):
         acc = values[t, side, pl.ds(pl.multiple_of(feat // 2 * fb, 8), fb), :]
-        for i in range(1, nf):
+        for i in range(nf - 1, 0, -1):
             sum_copy(g, t, i).wait_recv()
             acc = acc + f_in[g, t, i].astype(F32)
         return acc

time: 87.6 us -> 87.7 us (level)
  no operation moved by 1% of the time
where the time goes in v8:
time: 87.7 us; the launch traced here: 87.5 us
  Pallas kernels  82.7 us (94%)
  matrix products  3.52 us (4%)
    pallas_call x1, Pallas kernels, body(): pl.pallas_call(functools.partial(kernel, nz, nf, 1.0 / math.sqrt(all_rows...  82.7 us
    dot_general x1, matrix products, body(): jnp.einsum('lrd,lrf->ldf', a_all.reshape(layers, all_rows, depth), pre_gr...  3.52 us

profile of v8, /device:TPU:1, one launch (start us, length us, event | category | flops | bytes accessed | tf_op | source)
XLA Modules:
  0.0 87.5 jit_solution(6765511859764966910)
XLA Ops:
  0.6 82.7 %shard_map.86 = (bf16[5,2,1024]{2,1,0:T(2,128)(2,1)}, bf16[2,2,160,1024]{3,2,1,0:T(8,128)(2,1)}, bf16[2,2,160,256]{3,2,1,0:T(8,128)(2,1)}) custom-call(bf16[5,2,1024]{2,1,0:T(2,128)(2,1)} %act_hbm.1, bf16[5,2,1024]{2,1,0:T(2,128)(2,1)} %tgt_hbm.1, bf16[2,1024,256]{2,1,0:T(8,128)(2,1)} %enc_hbm.1, f32[2,256]{1,0:T(2,128)} %bias_hbm.1, ...), custom_call_target="tpu_custom_call" | custom-call | tf_op jit(solution)/shard_map/pallas_call | solution.py:437
  83.4 0.0 copy-start
  83.4 3.5 %fusion = f32[2,1024,256]{2,1,0:T(8,128)} fusion(bf16[2,320,1024]{2,1,0:T(8,128)(2,1)} %bitcast.5, bf16[2,320,256]{2,1,0:T(8,128)(2,1)} %bitcast.6), kind=kOutput, calls=%fused_computation | convolution fusion | flops 335544320 | bytes 3735552 | tf_op jit(solution)/shard_map/lrd,lrf->ldf/dot_general | solution.py:502
  86.9 0.0 copy-done
  86.9 0.6 copy.10
Async XLA Ops:
  83.4 3.5 %copy-start = (bf16[5,2,1024]{2,1,0:T(2,128)(2,1)S(1)}, bf16[5,2,1024]{2,1,0:T(2,128)(2,1)}, u32[]{:S(2)}) copy-start(bf16[5,2,1024]{2,1,0:T(2,128)(2,1)} %get-tuple-element.10) | copy-start | bytes 61444
